TPU v7x, 32 devices: a whole 2x2x4 slice. The times are simulated.
32 devices in a mesh: rep: 4 (over y, core), tp: 8 (over z, x).
Axes of the slice: x: 2, y: 2, z: 4, core: 2. Of those that a mesh axis runs over, the one named last changes fastest.
Arguments:
- tokens: bfloat16 [4096, 2048], P(('rep', 'tp')), may hold values from -6 to 6
- seg_ids: int32 [4096], replicated, may hold values from 0 to 15, never falling along the last dimension, each value on 1 to 1024 neighbouring positions
- expert_ids: int32 [4096, 8], P(('rep', 'tp')), may hold values from 0 to 31, all different within a row; in each aligned block of 128 rows (0 to 127, 128 to 255, ...) at most 48 rows name the same one
- gates: bfloat16 [4096, 8], P(('rep', 'tp')), may hold values from 0.099609375 to 0.59765625
- page_table: int32 [256], P(('rep', 'tp')), may hold values from 0 to 7, as said below
- attn_gain: float32 [2048], replicated, may hold values from 0.5 to 1.5
- q_gain: float32 [128], replicated, may hold values from 0.5 to 6, as said below
- key_norm_gain: float32 [128], replicated, may hold values from 0.5 to 6, as said below
- w_query: bfloat16 [2048, 4096], P(None, 'tp'), may hold values from -1 to 1
- w_keyval: bfloat16 [2048, 1024], replicated, may hold values from -1 to 1
- w_out: bfloat16 [4096, 2048], P('tp'), may hold values from -0.09375 to 0.09375
- moe_gain: float32 [2048], replicated, may hold values from 0.5 to 1.5
- w_gate_up: bfloat16 [32, 2048, 1536], P(('rep', 'tp')), may hold values from -0.125 to 0.125
- w_down: bfloat16 [32, 768, 2048], P(('rep', 'tp')), may hold values from -0.21875 to 0.21875
Outputs:
- hidden_out: bfloat16 [4096, 2048], P(('rep', 'tp'))
- cache: bfloat16 [256, 16, 1024], P(('rep', 'tp'))
Inputs may be any that keep to these rules, and one draw needn't show every extreme that they name: `seg_ids`: never falling; each request has at most 1024 tokens and some request has exactly 1024. `expert_ids`: a token's 8 experts differ; in the rows of one device no expert appears more than 48 times. `page_table`: the 8 entries of each device name each of its slots once. `q_gain`: positive. `key_norm_gain`: positive.
All inputs are finite; a program needn't handle non-finite values.
Results may differ from a plain program's by a relative error of at most 0.022.
Values may be sent and summed in bfloat16 or wider, within the bound.
No kernel may reach another device: no remote copies, remote signals or barrier semaphores. Data moves between devices by JAX's collectives and lax.ppermute only.
A program may use at most 128 MiB of HBM per device.

v0:
```python
import functools
import math

import jax
import jax.numpy as jnp
from jax import lax
from jax.experimental import pallas as pl
from jax.experimental.pallas import tpu as pltpu
from jax.sharding import PartitionSpec as P


def passed_along(block, axis, distance):
    devices = range(lax.axis_size(axis))
    route = [(i - distance, i) for i in devices if i - distance in devices]
    return lax.ppermute(block, axis, route)


def root_mean_norm(value_rows, gain):
    return (
        value_rows
        * lax.rsqrt(jnp.mean(value_rows * value_rows, axis=-1, keepdims=True) + 1e-06)
        * gain
    )


def apply_rotary(value_rows, token_positions):
    half_dim = value_rows.shape[-1] // 2
    frequency = jnp.exp(
        jnp.arange(half_dim, dtype=jnp.float32)
        * (-2.0 * math.log(1000000.0) / value_rows.shape[-1])
    )
    angles = token_positions[:, None] * frequency[None, :]
    cosine = jnp.cos(angles)[:, None, :]
    sine_part = jnp.sin(angles)[:, None, :]
    first = value_rows[..., :half_dim]
    second = value_rows[..., half_dim:]
    return jnp.concatenate(
        [first * cosine - second * sine_part, second * cosine + first * sine_part], axis=-1
    )


def general_body(
    tokens,
    seg_ids,
    expert_ids,
    gates,
    page_table,
    attn_gain,
    q_gain,
    key_norm_gain,
    w_query,
    w_keyval,
    w_out,
    moe_gain,
    w_gate_up,
    w_down,
):
    tok_rows, width = tokens.shape
    tp_count = lax.axis_size("tp")
    rep_count = lax.axis_size("rep")
    rep_index = lax.axis_index("rep")
    tp_index = lax.axis_index("tp")
    group_rows = tok_rows * tp_count
    head_dim = q_gain.shape[0]
    q_width = w_query.shape[1]
    heads_here = q_width // head_dim
    kv_heads = w_keyval.shape[1] // (2 * head_dim)
    kv_width = kv_heads * head_dim
    per_key_value = heads_here * tp_count // kv_heads
    own_head = tp_index * heads_here // per_key_value
    first_row = (rep_index * tp_count + tp_index) * tok_rows
    local_pos = (first_row + jnp.arange(tok_rows, dtype=jnp.int32)).astype(jnp.float32)
    normed = root_mean_norm(tokens.astype(jnp.float32), attn_gain).astype(jnp.bfloat16)
    key_value_rows = jnp.dot(normed, w_keyval, preferred_element_type=jnp.float32)
    rotary_output = apply_rotary(
        root_mean_norm(
            key_value_rows[:, :kv_width].reshape(tok_rows, kv_heads, head_dim), key_norm_gain
        ),
        local_pos,
    )
    stored_cache = jnp.concatenate(
        [rotary_output.reshape(tok_rows, kv_width), key_value_rows[:, kv_width:]], axis=1
    ).astype(jnp.bfloat16)
    page_count = page_table.shape[0]
    placement_matrix = (
        page_table[None, :] == jnp.arange(page_count, dtype=jnp.int32)[:, None]
    ).astype(jnp.bfloat16)
    cache = jnp.dot(
        placement_matrix, stored_cache.reshape(page_count, -1), preferred_element_type=jnp.float32
    )
    cache = cache.astype(jnp.bfloat16).reshape(page_count, tok_rows // page_count, 2 * kv_width)
    projected = jnp.dot(
        lax.all_gather(normed, "tp", axis=0, tiled=True),
        w_query,
        preferred_element_type=jnp.float32,
    )
    group_start = rep_index * group_rows
    group_pos = group_start + jnp.arange(group_rows, dtype=jnp.int32)
    group_posf = group_pos.astype(jnp.float32)
    query = root_mean_norm(projected.reshape(group_rows, heads_here, head_dim), q_gain)
    query = apply_rotary(query, group_posf).astype(jnp.bfloat16)
    gathered = lax.all_gather(stored_cache, "tp", axis=0, tiled=True)
    own_keys = lax.dynamic_slice_in_dim(gathered, own_head * head_dim, head_dim, 1)
    own_values = lax.dynamic_slice_in_dim(gathered, kv_width + own_head * head_dim, head_dim, 1)
    earlier_keys, earlier_values = passed_along((own_keys, own_values), "rep", 1)
    own_seg = lax.dynamic_slice_in_dim(seg_ids, group_start, group_rows, 0)
    earlier_seg = lax.dynamic_slice_in_dim(
        seg_ids, jnp.maximum(group_start - group_rows, 0), group_rows, 0
    )
    earlier_seg = jnp.where(rep_index > 0, earlier_seg, -1)
    keys_all = jnp.concatenate([earlier_keys, own_keys], axis=0)
    values_all = jnp.concatenate([earlier_values, own_values], axis=0)
    key_seg = jnp.concatenate([earlier_seg, own_seg], axis=0)
    key_pos = group_start - group_rows + jnp.arange(2 * group_rows, dtype=jnp.int32)
    block_rows = min(512, group_rows)
    block_count = group_rows // block_rows
    scale = head_dim ** (-0.5)

    def attend(inputs):
        block_query, block_pos, block_seg = inputs
        scores = (
            jnp.einsum("bhd,kd->hbk", block_query, keys_all, preferred_element_type=jnp.float32)
            * scale
        )
        allowed = (key_seg[None, :] == block_seg[:, None]) & (
            key_pos[None, :] <= block_pos[:, None]
        )
        scores = jnp.where(allowed[None], scores, -jnp.inf)
        largest = jnp.max(scores, axis=-1, keepdims=True)
        weights = jnp.exp(scores - largest)
        totals = jnp.sum(weights, axis=-1, keepdims=True)
        mixed = (
            jnp.einsum(
                "hbk,kd->hbd",
                weights.astype(jnp.bfloat16),
                values_all,
                preferred_element_type=jnp.float32,
            )
            / totals
        )
        return jnp.transpose(mixed.astype(jnp.bfloat16), (1, 0, 2)).reshape(
            block_rows, heads_here * head_dim
        )

    attended = lax.map(
        attend,
        (
            query.reshape(block_count, block_rows, heads_here, head_dim),
            group_pos.reshape(block_count, block_rows),
            own_seg.reshape(block_count, block_rows),
        ),
    )
    attended = attended.reshape(group_rows, heads_here * head_dim)
    rows = attended
    term = jnp.dot(rows, w_out, preferred_element_type=jnp.float32).astype(jnp.bfloat16)
    mixed_sum = lax.psum_scatter(
        lax.optimization_barrier(term).astype(jnp.float32).astype(jnp.bfloat16),
        "tp",
        scatter_dimension=0,
        tiled=True,
    ).astype(jnp.float32)
    residual = (tokens.astype(jnp.float32) + mixed_sum).astype(jnp.bfloat16)
    normed_moe = root_mean_norm(residual.astype(jnp.float32), moe_gain).astype(jnp.bfloat16)
    expert_count = rep_count * tp_count * w_gate_up.shape[0]
    top_count = expert_ids.shape[1]
    capacity = max(2, 3 * tok_rows * top_count // (2 * expert_count))
    hidden_units = w_down.shape[1]
    flat = expert_ids.reshape(-1)
    onehot = (flat[:, None] == jnp.arange(expert_count, dtype=jnp.int32)[None, :]).astype(jnp.int32)
    rank = jnp.sum((jnp.cumsum(onehot, axis=0) - 1) * onehot, axis=1)
    target = (flat * capacity + rank).reshape(tok_rows, top_count)
    match = (
        target[:, :, None] == jnp.arange(expert_count * capacity, dtype=jnp.int32)[None, None, :]
    )
    dispatch = jnp.any(match, axis=1).astype(jnp.bfloat16)
    combine = jnp.sum(jnp.where(match, gates[:, :, None].astype(jnp.float32), 0.0), axis=1).astype(
        jnp.bfloat16
    )
    outgoing = lax.dot_general(
        dispatch, normed_moe, (((0,), (0,)), ((), ())), preferred_element_type=jnp.float32
    )
    outgoing = outgoing.astype(jnp.bfloat16).reshape(expert_count, capacity, width)
    received = lax.all_to_all(outgoing, ("rep", "tp"), split_axis=0, concat_axis=0, tiled=True)
    rows = received.reshape(-1, width)
    gate_up = jnp.dot(rows, w_gate_up[0], preferred_element_type=jnp.float32)
    act = (jax.nn.silu(gate_up[:, :hidden_units]) * gate_up[:, hidden_units:]).astype(jnp.bfloat16)
    result = jnp.dot(act, w_down[0], preferred_element_type=jnp.float32).astype(jnp.bfloat16)
    returned = lax.all_to_all(
        result.reshape(received.shape), ("rep", "tp"), split_axis=0, concat_axis=0, tiled=True
    )
    combined = jnp.dot(
        combine,
        returned.reshape(expert_count * capacity, width),
        preferred_element_type=jnp.float32,
    )
    hidden_out = (residual.astype(jnp.float32) + combined).astype(jnp.bfloat16)
    return (hidden_out, cache)


KEY_BLOCK = 256
MASKED = -1e30


def moved(block, change):
    route = []
    for y in range(2):
        for core in range(2):
            for z in range(4):
                for x in range(2):
                    to_y, to_core, to_z, to_x = change(y, core, z, x)
                    route.append(
                        ((y * 2 + core) * 8 + z * 2 + x, (to_y * 2 + to_core) * 8 + to_z * 2 + to_x)
                    )
    return lax.ppermute(block, ("rep", "tp"), route)


def other_x(block):
    return moved(block, lambda y, core, z, x: (y, core, z, 1 - x))


def other_y(block):
    return moved(block, lambda y, core, z, x: (1 - y, core, z, x))


def other_core(block):
    return moved(block, lambda y, core, z, x: (y, 1 - core, z, x))


def across(block, over_y):
    if over_y:
        return moved(block, lambda y, core, z, x: (1 - y, 1 - core, z, x))
    return moved(block, lambda y, core, z, x: (y, 1 - core, z, 1 - x))


def other_z(block, k):
    return moved(block, lambda y, core, z, x: (y, core, z ^ k, x))


def sum_of(a, b):
    return (a.astype(jnp.float32) + b.astype(jnp.float32)).astype(jnp.bfloat16)


def after(value, earlier):
    return lax.optimization_barrier((value, earlier))[0]


def attention_kernel(
    first_slot, place, low, projected, gain, cosine, sine, start, kv_here, kv_side, kv_before, kv_before_side, out,
    keys, values, acc, peak, total,
):
    z, x, slot = place[0], place[1], first_slot + pl.program_id(0)
    rows = projected.shape[0]
    head = gain.shape[1]
    heads = projected.shape[1] // head
    half = head // 2

    @pl.when(pl.program_id(0) == 0)
    def _():
        for first, near, far in ((0, kv_before, kv_before_side), (8, kv_here, kv_side)):
            for k in range(4):
                at = jnp.bitwise_xor(z, k) * 2
                for source, shift in ((near, x), (far, 1 - x)):
                    row = pl.multiple_of((first + at + shift) * rows, rows)
                    keys[pl.ds(row, rows), :] = source[k, :rows, :head]
                    values[:, pl.ds(row, rows)] = source[k, :rows, head:].astype(jnp.float32).T.astype(jnp.bfloat16)

    gain_column = jnp.broadcast_to(gain[...], (rows, head)).T
    turned = []
    for h in range(heads):
        q = projected[:, h * head : (h + 1) * head].T
        q = q * lax.rsqrt(jnp.mean(q * q, axis=0, keepdims=True) + 1e-06) * gain_column
        first, second = q[:half], q[half:]
        turned.append(
            jnp.concatenate(
                [first * cosine[0] - second * sine[0], second * cosine[0] + first * sine[0]], axis=0
            )
        )
    query = (jnp.concatenate(turned, axis=1) * (head**-0.5 * math.log2(math.e))).astype(jnp.bfloat16)
    acc[...] = jnp.zeros_like(acc)
    total[...] = jnp.zeros_like(total)
    peak[...] = jnp.full_like(peak, MASKED)
    position = (8 + jnp.bitwise_xor(z, slot) * 2 + x) * rows
    own_position = position + lax.broadcasted_iota(jnp.int32, (KEY_BLOCK, rows), 1)
    own_start = start[0]

    def step(j, _):
        row = pl.multiple_of(j * KEY_BLOCK, KEY_BLOCK)
        scores = jnp.dot(keys[pl.ds(row, KEY_BLOCK), :], query, preferred_element_type=jnp.float32)
        key_position = row + lax.broadcasted_iota(jnp.int32, (KEY_BLOCK, rows), 0)
        allowed = (key_position >= own_start) & (key_position <= own_position)
        scores = jnp.concatenate(
            [jnp.where(allowed, scores[:, h * rows : (h + 1) * rows], MASKED) for h in range(heads)], axis=1
        )
        largest = jnp.maximum(peak[...], jnp.max(scores, axis=0, keepdims=True))
        fade = jnp.exp2(peak[...] - largest)
        weights = jnp.exp2(scores - largest)
        total[...] = total[...] * fade + jnp.sum(weights, axis=0, keepdims=True)
        acc[...] = acc[...] * fade + jnp.dot(
            values[:, pl.ds(row, KEY_BLOCK)], weights.astype(jnp.bfloat16), preferred_element_type=jnp.float32
        )
        peak[...] = largest
        return 0

    lax.fori_loop(low[slot], (position + rows - 1) // KEY_BLOCK + 1, step, 0)
    mixed = acc[...] / total[...]
    for h in range(heads):
        out[:, h * head : (h + 1) * head] = mixed[:, h * rows : (h + 1) * rows].T.astype(out.dtype)


def attend_slots(first_slot, place, low, projected, q_gain, cosine, sine, start, kv):
    rows = start.shape[2]
    slots = projected.shape[0] // rows
    head = q_gain.shape[0]
    width = projected.shape[1]
    whole = lambda *shape: pl.BlockSpec(shape, lambda s, *_: (0,) * len(shape))
    return pl.pallas_call(
        functools.partial(attention_kernel, first_slot),
        grid_spec=pltpu.PrefetchScalarGridSpec(
            num_scalar_prefetch=2,
            grid=(slots,),
            in_specs=[
                pl.BlockSpec((rows, width), lambda s, *_: (s, 0)),
                whole(1, head),
                pl.BlockSpec((1, head // 2, rows), lambda s, *_: (first_slot + s, 0, 0)),
                pl.BlockSpec((1, head // 2, rows), lambda s, *_: (first_slot + s, 0, 0)),
                pl.BlockSpec((1, 1, rows), lambda s, *_: (first_slot + s, 0, 0)),
            ]
            + [whole(*part.shape) for part in kv],
            out_specs=pl.BlockSpec((rows, width), lambda s, *_: (s, 0)),
            scratch_shapes=[
                pltpu.VMEM((16 * rows, head), jnp.bfloat16),
                pltpu.VMEM((head, 16 * rows), jnp.bfloat16),
                pltpu.VMEM((head, width // head * rows), jnp.float32),
                pltpu.VMEM((1, width // head * rows), jnp.float32),
                pltpu.VMEM((1, width // head * rows), jnp.float32),
            ],
        ),
        out_shape=jax.ShapeDtypeStruct((slots * rows, width), jnp.bfloat16),
        compiler_params=pltpu.CompilerParams(vmem_limit_bytes=40 * 2**20),
        cost_estimate=pl.CostEstimate(
            flops=4 * slots * rows * width * 4 * rows,
            bytes_accessed=8 * 2**20,
            transcendentals=slots * width * rows,
        ),
        name="attention",
    )(place, low, projected, q_gain.reshape(1, head), cosine, sine, start, *kv)


def keyval_kernel(tokens, gain, key_gain, cosine, sine, w_key, w_value, out, normed):
    @pl.when(pl.program_id(0) == 0)
    def _():
        normed[...] = root_mean_norm(tokens[...].astype(jnp.float32), gain[...]).astype(jnp.bfloat16)

    head = key_gain.shape[1]
    half = head // 2
    k = jnp.dot(normed[...], w_key[...], preferred_element_type=jnp.float32).T
    k = k * lax.rsqrt(jnp.mean(k * k, axis=0, keepdims=True) + 1e-06)
    k = k * jnp.broadcast_to(key_gain[...], (normed.shape[0], head)).T
    first, second = k[:half], k[half:]
    k = jnp.concatenate(
        [first * cosine[0] - second * sine[0], second * cosine[0] + first * sine[0]], axis=0
    )
    out[0, :, :head] = k.T.astype(out.dtype)
    v = jnp.dot(normed[...], w_value[...], preferred_element_type=jnp.float32)
    out[0, :, head:] = v.astype(out.dtype)


def keyval_by_head(tokens, attn_gain, key_norm_gain, cosine, sine, w_keyval):
    rows, width = tokens.shape
    head = key_norm_gain.shape[0]
    heads = w_keyval.shape[1] // (2 * head)
    whole = lambda *shape: pl.BlockSpec(shape, lambda h: (0,) * len(shape))
    return pl.pallas_call(
        keyval_kernel,
        grid=(heads,),
        in_specs=[
            whole(rows, width),
            whole(1, width),
            whole(1, head),
            pl.BlockSpec((1, head // 2, rows), lambda h: (0, 0, 0)),
            pl.BlockSpec((1, head // 2, rows), lambda h: (0, 0, 0)),
            pl.BlockSpec((width, head), lambda h: (0, h)),
            pl.BlockSpec((width, head), lambda h: (0, heads + h)),
        ],
        out_specs=pl.BlockSpec((1, rows, 2 * head), lambda h: (h, 0, 0)),
        out_shape=jax.ShapeDtypeStruct((heads, rows, 2 * head), jnp.bfloat16),
        scratch_shapes=[pltpu.VMEM((rows, width), jnp.bfloat16)],
        compiler_params=pltpu.CompilerParams(vmem_limit_bytes=60 * 2**20),
        cost_estimate=pl.CostEstimate(
            flops=2 * rows * width * w_keyval.shape[1], bytes_accessed=5 * 2**20, transcendentals=0
        ),
        name="keyval",
    )(tokens, attn_gain.reshape(1, width), key_norm_gain.reshape(1, head), cosine, sine, w_keyval, w_keyval)


def grid_body(
    tokens,
    seg_ids,
    expert_ids,
    gates,
    page_table,
    attn_gain,
    q_gain,
    key_norm_gain,
    w_query,
    w_keyval,
    w_out,
    moe_gain,
    w_gate_up,
    w_down,
):
    rows, width = tokens.shape
    head = q_gain.shape[0]
    kv_heads = w_keyval.shape[1] // (2 * head)
    kv_width = kv_heads * head
    rep, tp = lax.axis_index("rep"), lax.axis_index("tp")
    y, core, z, x = rep // 2, rep % 2, tp // 2, tp % 2
    group_rows = 8 * rows
    group_start = rep * group_rows
    slots = range(4)

    slot_start = [group_start + ((z ^ k) * 2 + x) * rows for k in slots]
    slot_position = jnp.stack([at + jnp.arange(rows, dtype=jnp.int32) for at in slot_start])
    frequency = jnp.exp(
        jnp.arange(head // 2, dtype=jnp.float32) * (-2.0 * math.log(1000000.0) / head)
    )
    angles = frequency[None, :, None] * slot_position.astype(jnp.float32)[:, None, :]
    cosine, sine = jnp.cos(angles), jnp.sin(angles)

    by_head = keyval_by_head(tokens, attn_gain, key_norm_gain, cosine, sine, w_keyval)
    part = w_query.shape[1] // 4
    quarter = y * 2 + core
    far = other_z(tokens, 2)
    query_x = other_x(lax.dynamic_slice_in_dim(w_query, quarter * part, part, 1))
    by_head, late_segs, query_x, w_out = lax.optimization_barrier((by_head, seg_ids, query_x, w_out))
    out_x = other_x(lax.dynamic_slice_in_dim(w_out, quarter * part, part, 0))

    top = expert_ids.shape[1]
    routes = jnp.concatenate([expert_ids.T.astype(jnp.bfloat16), gates.T], axis=0)
    routes = jnp.concatenate([routes, other_y(routes)], axis=1)
    pick = lambda h: jnp.concatenate(
        [lax.dynamic_index_in_dim(by_head, h, 0, keepdims=False), routes], axis=0
    )
    kv_parts = [other_z(pick(z ^ k), k) for k in (1, 2, 3)]
    query_y = other_y(after(query_x, kv_parts[0]))
    kv_here = jnp.stack([pick(z)] + kv_parts)
    kv_here, out_x, far, w_query, w_out = lax.optimization_barrier((kv_here, out_x, far, w_query, w_out))
    kv_before, kv_side = passed_along(kv_here, "rep", 1), other_x(kv_here)
    farther, out_y = other_z(far, 1), other_y(out_x)
    kv_side, query_y = lax.optimization_barrier((kv_side, query_y))
    kv_before_side = passed_along(kv_side, "rep", 1)
    query_two = jnp.concatenate([query_x, query_y], axis=1)
    query_far = other_core(query_two)
    kv_before, query_far, farther, out_y = lax.optimization_barrier(
        (kv_before, query_far, farther, out_y)
    )
    w_query_wide = jnp.concatenate([w_query, query_two, query_far], axis=1)
    out_two = jnp.concatenate([out_x, out_y], axis=0)
    near = other_z(after(tokens, farther), 1)
    w_out_wide = jnp.concatenate([w_out, out_two, other_core(out_two)], axis=0)
    raw = [tokens, near, far, farther]

    pages = page_table.shape[0]
    stored = jnp.transpose(by_head.reshape(kv_heads, rows, 2, head), (1, 2, 0, 3))
    placing = (page_table[None, :] == jnp.arange(pages, dtype=jnp.int32)[:, None]).astype(jnp.bfloat16)
    cache = jnp.dot(placing, stored.reshape(pages, -1), preferred_element_type=jnp.float32)
    cache = cache.astype(jnp.bfloat16).reshape(pages, rows // pages, 2 * kv_width)

    slot_seg = jnp.concatenate(
        [lax.dynamic_slice_in_dim(late_segs, at, rows, 0) for at in slot_start]
    )
    starts = jnp.sum((late_segs[None, :] < slot_seg[:, None]).astype(jnp.int32), axis=1)
    starts = (starts - (group_start - group_rows)).reshape(4, 1, rows)
    low = starts[:, 0, 0] // KEY_BLOCK

    def projection(first):
        lines = jnp.concatenate(raw[first : first + 2], axis=0).astype(jnp.float32)
        lines = root_mean_norm(lines, attn_gain).astype(jnp.bfloat16)
        return jnp.dot(lines, w_query_wide, preferred_element_type=jnp.float32)

    def attended(first, projected):
        return attend_slots(
            first,
            jnp.stack([z, x]),
            low,
            projected,
            q_gain,
            cosine,
            sine,
            starts,
            (kv_here, kv_side, kv_before, kv_before_side),
        )

    def term_of(part):
        term = jnp.dot(part, w_out_wide, preferred_element_type=jnp.float32).astype(jnp.bfloat16)
        return term[:rows], term[rows:]

    attended_far = attended(2, projection(2))
    term_2, term_3 = term_of(attended_far)
    term_2, raw[1] = lax.optimization_barrier((term_2, near))
    far_3 = other_z(term_3, 1)
    far = other_z(sum_of(term_2, far_3), 2)
    term_0, term_1 = term_of(attended(0, after(projection(0), term_3)))
    near = other_z(term_1, 1)
    mixed_sum = term_0.astype(jnp.float32) + near.astype(jnp.float32) + far.astype(jnp.float32)
    residual = (tokens.astype(jnp.float32) + mixed_sum).astype(jnp.bfloat16)
    normed_moe = root_mean_norm(residual.astype(jnp.float32), moe_gain).astype(jnp.bfloat16)

    turned = (False, True, False, True)
    routes, over_y = kv_here[:, rows:, :rows], kv_here[:, rows:, rows:]
    over_x, corner_routes = kv_side[:, rows:, :rows], kv_side[0, rows:, rows:]
    capacity = max(2, 3 * rows * top // (2 * 32))
    pair = 2 * capacity
    mine = [rep * 8 + tp, (rep ^ 1) * 8 + tp]
    earlier = (jnp.arange(rows)[:, None] < jnp.arange(rows)[None, :]).astype(jnp.bfloat16)

    def matrices(blocks, experts):
        blocks = blocks.reshape(blocks.shape[:2] + (2, top, rows))
        experts = experts.astype(jnp.bfloat16)
        hits = blocks[:, :, 0][:, :, None] == experts[:, None, :, None, None]
        weight = jnp.sum(jnp.where(hits, blocks[:, :, 1][:, :, None].astype(jnp.float32), 0.0), axis=3)
        hit = jnp.any(hits, axis=3)
        place = jnp.dot(
            hit.reshape(-1, rows).astype(jnp.bfloat16), earlier, preferred_element_type=jnp.float32
        ).reshape(hit.shape)
        chosen = (
            place[..., None, :].astype(jnp.int32) == jnp.arange(capacity, dtype=jnp.int32)[:, None]
        ) & hit[..., None, :]
        weighted = jnp.where(chosen, weight[..., None, :], 0.0).astype(jnp.bfloat16)
        flat = hit.shape[:2] + (-1, rows)
        return chosen.astype(jnp.bfloat16).reshape(flat), weighted.reshape(flat)

    pairs = [jnp.stack([routes[k], (over_y if turned[k] else over_x)[k]]) for k in slots]
    theirs = [[e ^ 1 if turned[k] else e ^ 16 for e in mine] for k in slots]
    chosen, weighted = matrices(
        jnp.stack(pairs + [jnp.stack([over_y[0], corner_routes])]),
        jnp.stack([jnp.stack(mine + others) for others in theirs + [mine]]),
    )
    chosen_0 = jnp.concatenate([chosen[0, :, :pair], chosen[4, :, :pair]], axis=0)

    def experts_of(slot_rows_in):
        gate_up = jnp.dot(slot_rows_in, w_gate_up[0], preferred_element_type=jnp.float32)
        hidden = w_down.shape[1]
        act = (jax.nn.silu(gate_up[:, :hidden]) * gate_up[:, hidden:]).astype(jnp.bfloat16)
        return jnp.dot(act, w_down[0], preferred_element_type=jnp.float32).astype(jnp.bfloat16)

    together = lambda *values: lax.optimization_barrier(values)

    def picks(k, block, side):
        picked = lax.dot_general(
            chosen[k], jnp.stack([block, side]), (((2,), (1,)), ((0,), (0,))), preferred_element_type=jnp.float32
        ).astype(jnp.bfloat16)
        return picked[:, :pair], picked[:, pair:]

    half = rows // 2
    near, far = other_z(normed_moe, 1), other_z(normed_moe, 2)
    side_x, side_y = together(other_x(normed_moe), other_y(normed_moe))
    near, far, *corner = together(near, far, other_y(side_x[:half]), other_x(side_y[half:]))
    side_1, side_2, farther = other_y(near), other_x(far), other_z(far, 1)
    corner = jnp.concatenate(corner, axis=0)
    picked_0 = lax.dot_general(
        chosen_0,
        jnp.stack([normed_moe, side_x, side_y, corner]),
        (((2,), (1,)), ((0,), (0,))),
        preferred_element_type=jnp.float32,
    ).astype(jnp.bfloat16)
    side_2, farther, picked_0 = together(side_2, farther, picked_0)
    mine_2, theirs_2 = picks(2, far, side_2)
    side_3 = other_y(farther)
    side_1, mine_2, theirs_2 = together(side_1, mine_2, theirs_2)
    mine_1, theirs_1 = picks(1, near, side_1)
    theirs_1 = other_x(theirs_1)

    def over_second(to_y, to_y_across, to_x, to_x_across):
        return together(
            other_y(to_y), across(to_y_across, True), other_x(to_x), across(to_x_across, False)
        )

    def experts_on(*parts):
        return experts_of(jnp.concatenate(parts, axis=0).reshape(-1, width)).reshape(-1, capacity, width)

    kept = lambda *parts: jnp.concatenate([part[:, :capacity] for part in parts], axis=0)
    traded = lambda *parts: other_core(jnp.concatenate([part[:, capacity:] for part in parts], axis=0))
    result_0 = experts_on(kept(picked_0), traded(picked_0))
    result_12 = experts_on(kept(mine_1, mine_2), traded(mine_1, mine_2))
    side_3, theirs_2, result_0, result_12 = together(side_3, theirs_2, result_0, result_12)
    mine_3, theirs_3 = picks(3, farther, side_3)
    theirs_3, theirs_1 = together(theirs_3, theirs_1)
    late = traded(mine_3, theirs_1)
    got = over_second(
        theirs_2[:, :capacity], theirs_2[:, capacity:], theirs_3[:, :capacity], theirs_3[:, capacity:]
    )
    *got, late = together(*got, late)
    got, late = together(experts_on(*got), late)
    result_31 = experts_on(kept(mine_3, theirs_1), late)
    both = lambda result: jnp.concatenate([result[:4], other_core(result[4:])], axis=1)
    here_1, here_2 = jnp.split(both(result_12), 2)
    here_3, there_1 = jnp.split(both(result_31), 2)

    def summed(k, here, there):
        total = lax.dot_general(
            weighted[k],
            jnp.concatenate([here, there], axis=1),
            (((1,), (1,)), ((0,), (0,))),
            preferred_element_type=jnp.float32,
        ).astype(jnp.bfloat16)
        return total[0], total[1]

    here_0, there_0 = jnp.split(both(result_0), 2)
    there = over_second(got[:2], got[2:4], got[4:6], got[6:])
    there_2, there_3 = jnp.concatenate(there[:2], axis=1), jnp.concatenate(there[2:], axis=1)
    (own_2, side_2), (own_3, side_3) = summed(2, here_2, there_2), summed(3, here_3, there_3)
    side_2, side_3, there_0, there_1 = together(other_x(side_2), other_y(side_3), there_0, there_1)
    far_3 = other_z(sum_of(own_3, side_3), 1)
    there_0, there_1 = together(other_y(there_0), other_x(there_1))
    (own_0, side_0), (own_1, side_1) = summed(0, here_0, there_0), summed(1, here_1, there_1)
    far = own_2.astype(jnp.float32) + side_2.astype(jnp.float32) + far_3.astype(jnp.float32)
    far = other_z(far.astype(jnp.bfloat16), 2)
    side_0 = other_x(side_0)
    near = [
        other_z(sum_of(own_1[part], other_y(side_1[part])), 1) for part in (slice(0, half), slice(half, rows))
    ]
    near = jnp.concatenate(near, axis=0)
    combined = residual.astype(jnp.float32)
    for value in (far, near, own_0, side_0):
        combined = combined + value.astype(jnp.float32)
    return (combined.astype(jnp.bfloat16), cache)


def solution(mesh):
    in_specs = (
        P(("rep", "tp"), None),
        P(),
        P(("rep", "tp"), None),
        P(("rep", "tp"), None),
        P(("rep", "tp")),
        P(),
        P(),
        P(),
        P(None, "tp"),
        P(),
        P("tp", None),
        P(),
        P(("rep", "tp"), None, None),
        P(("rep", "tp"), None, None),
    )
    out_specs = (P(("rep", "tp"), None), P(("rep", "tp"), None, None))
    body = grid_body if (mesh.shape["rep"], mesh.shape["tp"]) == (4, 8) else general_body
    return jax.shard_map(body, mesh=mesh, in_specs=in_specs, out_specs=out_specs, check_vma=False)
```

profile of v0, /device:TPU:0, one launch (start us, length us, event | category | flops | bytes accessed | tf_op | source)
XLA Modules:
  0.0 288.5 jit_solution(16998170446891255391)
XLA Ops:
  0.7 2.0 constant_dynamic-slice_fusion.1
  2.7 2.9 %collective-permute-start = (bf16[2048,128]{1,0:T(8,128)(2,1)}, bf16[2048,128]{1,0:T(8,128)(2,1)}, u32[]{:S(2)}, u32[]{:S(2)}) collective-permute-start(bf16[2048,128]{1,0:T(8,128)(2,1)} %constant_dynamic-slice_fusion.1), channel_id=1, source_target_pairs={{0,1},{1,0},{2,3},{3,2},{4,5},{5,4},{6,7},{7,6},{8,9},{9,8},{10,11... | collective-permute-start | bytes 1572872 | tf_op jit(solution)/shard_map/ppermute | solution.py:214
  8.5 2.6 collective-permute-start.6
  12.7 5.2 %keyval.1 = bf16[4,128,256]{2,1,0:T(8,128)(2,1)} custom-call(bf16[128,2048]{1,0:T(8,128)(2,1)} %tokens.1, f32[1,2048]{1,0:T(1,128)} %bitcast.225, f32[1,128]{1,0:T(1,128)} %bitcast.226, f32[4,64,128]{2,1,0:T(8,128)} %get-tuple-element.196.cosine, f32[4,64,128]{2,1,0:T(8,128)} %get-tuple-element.195.sine, bf16[2048,1024]{1,0:T(8,128)(2,1)} %w_value.1, ...), custom_call_target="tpu_custom_call" | custom-call | flops 536870912 | bytes 5242880 | tf_op jit(solution)/shard_map/keyval/pallas_call | solution.py:373
  20.1 3.8 %collective-permute-start.4 = (bf16[144,256]{1,0:T(8,128)(2,1)S(1)}, bf16[144,256]{1,0:T(8,128)(2,1)S(1)}, u32[]{:S(2)}, u32[]{:S(2)}) collective-permute-start(bf16[144,256]{1,0:T(8,128)(2,1)S(1)} %get-tuple-element.194), channel_id=1, source_target_pairs={{0,6},{1,7},{2,4},{3,5},{4,2},{5,3},{6,0},{7,1},{8,14},{9,15},{10,... | collective-permute-start | bytes 221192 | tf_op jit(solution)/shard_map/ppermute | solution.py:214
  27.5 8.7 %collective-permute-done.2 = bf16[144,256]{1,0:T(8,128)(2,1)S(1)} collective-permute-done((bf16[144,256]{1,0:T(8,128)(2,1)S(1)}, bf16[144,256]{1,0:T(8,128)(2,1)S(1)}, u32[]{:S(2)}, u32[]{:S(2)}) %collective-permute-start.2) | collective-permute-done | bytes 73760 | tf_op jit(solution)/shard_map/ppermute | solution.py:214
  36.5 3.8 %collective-permute-done.3 = bf16[144,256]{1,0:T(8,128)(2,1)S(1)} collective-permute-done((bf16[144,256]{1,0:T(8,128)(2,1)S(1)}, bf16[144,256]{1,0:T(8,128)(2,1)S(1)}, u32[]{:S(2)}, u32[]{:S(2)}) %collective-permute-start.3) | collective-permute-done | bytes 73760 | tf_op jit(solution)/shard_map/ppermute | solution.py:214
  46.1 1.9 collective-permute-done.8.kv_side
  49.2 2.4 collective-permute-start.13
  51.9 6.7 %collective-permute-done.11 = bf16[128,2048]{1,0:T(8,128)(2,1)S(1)} collective-permute-done((bf16[128,2048]{1,0:T(8,128)(2,1)}, bf16[128,2048]{1,0:T(8,128)(2,1)S(1)}, u32[]{:S(2)}, u32[]{:S(2)}) %collective-permute-start.11) | collective-permute-done | bytes 524320 | tf_op jit(solution)/shard_map/ppermute | solution.py:214
  62.5 2.4 fusion.72.projected
  65.0 5.3 %attention.2 = bf16[256,1024]{1,0:T(8,128)(2,1)S(1)} custom-call(s32[2]{0:T(128)S(1)} %pad_add_fusion.1.place, s32[4]{0:T(128)S(1)} %and_select_fusion.low, f32[256,1024]{1,0:T(8,128)S(1)} %fusion.72.projected, f32[1,128]{1,0:T(1,128)S(1)} %bitcast.192, f32[4,64,128]{2,1,0:T(8,128)S(1)} %copy-done.2, f32[4,64,128]{2,1,0:T(8,128)S(1)} %copy-done.1, ...), custom_call_target="tpu_custom_call" | custom-call | flops 536870912 | bytes 8388608 | tf_op jit(solution)/shard_map/attention/pallas_call | solution.py:316
  72.7 3.2 %collective-permute-done.15 = bf16[128,2048]{1,0:T(8,128)(2,1)S(1)} collective-permute-done((bf16[128,2048]{1,0:T(8,128)(2,1)S(1)}, bf16[128,2048]{1,0:T(8,128)(2,1)S(1)}, u32[]{:S(2)}, u32[]{:S(2)}) %collective-permute-start.15) | collective-permute-done | bytes 524320 | tf_op jit(solution)/shard_map/ppermute | solution.py:214
  77.5 4.1 %attention.3 = bf16[256,1024]{1,0:T(8,128)(2,1)S(1)} custom-call(s32[2]{0:T(128)S(1)} %pad_add_fusion.1.place, s32[4]{0:T(128)S(1)} %and_select_fusion.low, f32[256,1024]{1,0:T(8,128)S(1)} %fusion.70.projected, f32[1,128]{1,0:T(1,128)S(1)} %bitcast.193, f32[4,64,128]{2,1,0:T(8,128)S(1)} %copy-done.2, f32[4,64,128]{2,1,0:T(8,128)S(1)} %copy-done.1, ...), custom_call_target="tpu_custom_call" | custom-call | flops 536870912 | bytes 8388608 | tf_op jit(solution)/shard_map/attention/pallas_call | solution.py:316
  84.2 2.9 %collective-permute-done.17 = bf16[128,2048]{1,0:T(8,128)(2,1)S(1)} collective-permute-done((bf16[128,2048]{1,0:T(8,128)(2,1)S(1)}, bf16[128,2048]{1,0:T(8,128)(2,1)S(1)}, u32[]{:S(2)}, u32[]{:S(2)}) %collective-permute-start.17) | collective-permute-done | bytes 524320 | tf_op jit(solution)/shard_map/ppermute | solution.py:214
  87.3 3.3 %collective-permute-start.18 = (bf16[128,2048]{1,0:T(8,128)(2,1)S(1)}, bf16[128,2048]{1,0:T(8,128)(2,1)S(1)}, u32[]{:S(2)}, u32[]{:S(2)}) collective-permute-start(bf16[128,2048]{1,0:T(8,128)(2,1)S(1)} %add_convert_fusion.1), channel_id=1, source_target_pairs={{0,4},{1,5},{2,6},{3,7},{4,0},{5,1},{6,2},{7,3},{8,12},{9,13},{10,... | collective-permute-start | bytes 1572872 | tf_op jit(solution)/shard_map/ppermute | solution.py:214
  91.0 16.9 %collective-permute-done.16 = bf16[128,2048]{1,0:T(8,128)(2,1)S(1)} collective-permute-done((bf16[128,2048]{1,0:T(8,128)(2,1)S(1)}, bf16[128,2048]{1,0:T(8,128)(2,1)S(1)}, u32[]{:S(2)}, u32[]{:S(2)}) %collective-permute-start.16) | collective-permute-done | bytes 524320 | tf_op jit(solution)/shard_map/ppermute | solution.py:214
  107.9 5.1 %collective-permute-done.18 = bf16[128,2048]{1,0:T(8,128)(2,1)S(1)} collective-permute-done((bf16[128,2048]{1,0:T(8,128)(2,1)S(1)}, bf16[128,2048]{1,0:T(8,128)(2,1)S(1)}, u32[]{:S(2)}, u32[]{:S(2)}) %collective-permute-start.18) | collective-permute-done | bytes 524320 | tf_op jit(solution)/shard_map/ppermute | solution.py:214
  117.0 2.5 collective-permute-start.20
  119.8 5.3 %collective-permute-done.21 = bf16[128,2048]{1,0:T(8,128)(2,1)S(1)} collective-permute-done((bf16[128,2048]{1,0:T(8,128)(2,1)S(1)}, bf16[128,2048]{1,0:T(8,128)(2,1)S(1)}, u32[]{:S(2)}, u32[]{:S(2)}) %collective-permute-start.21) | collective-permute-done | bytes 524320 | tf_op jit(solution)/shard_map/ppermute | solution.py:214
  125.0 2.3 collective-permute-done.22
  129.2 8.2 %collective-permute-done.19 = bf16[128,2048]{1,0:T(8,128)(2,1)S(1)} collective-permute-done((bf16[128,2048]{1,0:T(8,128)(2,1)S(1)}, bf16[128,2048]{1,0:T(8,128)(2,1)S(1)}, u32[]{:S(2)}, u32[]{:S(2)}) %collective-permute-start.19) | collective-permute-done | bytes 524320 | tf_op jit(solution)/shard_map/ppermute | solution.py:214
  137.4 2.9 %collective-permute-done.20 = bf16[128,2048]{1,0:T(8,128)(2,1)S(1)} collective-permute-done((bf16[128,2048]{1,0:T(8,128)(2,1)S(1)}, bf16[128,2048]{1,0:T(8,128)(2,1)S(1)}, u32[]{:S(2)}, u32[]{:S(2)}) %collective-permute-start.20) | collective-permute-done | bytes 524320 | tf_op jit(solution)/shard_map/ppermute | solution.py:214
  141.2 1.8 collective-permute-start.28
  143.6 5.9 %collective-permute-done.25 = bf16[128,2048]{1,0:T(8,128)(2,1)S(1)} collective-permute-done((bf16[128,2048]{1,0:T(8,128)(2,1)S(1)}, bf16[128,2048]{1,0:T(8,128)(2,1)S(1)}, u32[]{:S(2)}, u32[]{:S(2)}) %collective-permute-start.25) | collective-permute-done | bytes 524320 | tf_op jit(solution)/shard_map/ppermute | solution.py:214
  152.4 1.8 collective-permute-start.27
  156.3 2.7 fusion.6
  159.2 2.7 fusion.4
  164.8 2.1 collective-permute-done.27
  166.9 1.8 collective-permute-start.32
  169.6 4.8 %collective-permute-done.34 = bf16[2,96,2048]{2,1,0:T(8,128)(2,1)S(1)} collective-permute-done((bf16[2,96,2048]{2,1,0:T(8,128)(2,1)S(1)}, bf16[2,96,2048]{2,1,0:T(8,128)(2,1)S(1)}, u32[]{:S(2)}, u32[]{:S(2)}) %collective-permute-start.34) | collective-permute-done | bytes 786464 | tf_op jit(solution)/shard_map/ppermute | solution.py:214
  179.0 6.4 %collective-permute-done.33 = bf16[2,48,2048]{2,1,0:T(8,128)(2,1)S(1)} collective-permute-done((bf16[2,48,2048]{2,1,0:T(8,128)(2,1)S(1)}, bf16[2,48,2048]{2,1,0:T(8,128)(2,1)S(1)}, u32[]{:S(2)}, u32[]{:S(2)}) %collective-permute-start.33) | collective-permute-done | bytes 393248 | tf_op jit(solution)/shard_map/ppermute | solution.py:214
  186.6 5.9 %collective-permute-done.36 = bf16[2,48,2048]{2,1,0:T(8,128)(2,1)S(1)} collective-permute-done((bf16[2,48,2048]{2,1,0:T(8,128)(2,1)S(1)}, bf16[2,48,2048]{2,1,0:T(8,128)(2,1)S(1)}, u32[]{:S(2)}, u32[]{:S(2)}) %collective-permute-start.36) | collective-permute-done | bytes 393248 | tf_op jit(solution)/shard_map/ppermute | solution.py:214
  192.7 2.6 fusion.2
  197.2 1.9 collective-permute-start.39
  200.8 2.7 fusion
  205.8 3.1 %collective-permute-done.38 = bf16[2,48,2048]{2,1,0:T(8,128)(2,1)S(1)} collective-permute-done((bf16[2,48,2048]{2,1,0:T(8,128)(2,1)S(1)}, bf16[2,48,2048]{2,1,0:T(8,128)(2,1)S(1)}, u32[]{:S(2)}, u32[]{:S(2)}) %collective-permute-start.38) | collective-permute-done | bytes 393248 | tf_op jit(solution)/shard_map/ppermute | solution.py:214
  209.0 8.1 %collective-permute-done.39 = bf16[2,48,2048]{2,1,0:T(8,128)(2,1)S(1)} collective-permute-done((bf16[2,48,2048]{2,1,0:T(8,128)(2,1)S(1)}, bf16[2,48,2048]{2,1,0:T(8,128)(2,1)S(1)}, u32[]{:S(2)}, u32[]{:S(2)}) %collective-permute-start.39) | collective-permute-done | bytes 393248 | tf_op jit(solution)/shard_map/ppermute | solution.py:214
  221.0 11.8 %collective-permute-done.42 = bf16[128,2048]{1,0:T(8,128)(2,1)S(1)} collective-permute-done((bf16[128,2048]{1,0:T(8,128)(2,1)S(1)}, bf16[128,2048]{1,0:T(8,128)(2,1)S(1)}, u32[]{:S(2)}, u32[]{:S(2)}) %collective-permute-start.42) | collective-permute-done | bytes 524320 | tf_op jit(solution)/shard_map/ppermute | solution.py:214
  236.7 11.4 %collective-permute-done.46 = bf16[128,2048]{1,0:T(8,128)(2,1)S(1)} collective-permute-done((bf16[128,2048]{1,0:T(8,128)(2,1)S(1)}, bf16[128,2048]{1,0:T(8,128)(2,1)S(1)}, u32[]{:S(2)}, u32[]{:S(2)}) %collective-permute-start.46) | collective-permute-done | bytes 524320 | tf_op jit(solution)/shard_map/ppermute | solution.py:214
  249.1 2.6 collective-permute-start.47
  251.7 2.5 collective-permute-done.48
  259.2 5.4 %collective-permute-done.50 = bf16[64,2048]{1,0:T(8,128)(2,1)S(1)} collective-permute-done((bf16[64,2048]{1,0:T(8,128)(2,1)S(1)}, bf16[64,2048]{1,0:T(8,128)(2,1)S(1)}, u32[]{:S(2)}, u32[]{:S(2)}) %collective-permute-start.50) | collective-permute-done | bytes 262176 | tf_op jit(solution)/shard_map/ppermute | solution.py:214
  264.6 2.8 collective-permute-done.52
  271.1 2.0 copy.31
  275.4 4.7 %collective-permute-done.53 = bf16[64,2048]{1,0:T(8,128)(2,1)} collective-permute-done((bf16[64,2048]{1,0:T(8,128)(2,1)}, bf16[64,2048]{1,0:T(8,128)(2,1)}, u32[]{:S(2)}, u32[]{:S(2)}) %collective-permute-start.53) | collective-permute-done | bytes 262176 | tf_op jit(solution)/shard_map/ppermute | solution.py:214
  280.1 5.5 %collective-permute-done.51 = bf16[64,2048]{1,0:T(8,128)(2,1)} collective-permute-done((bf16[64,2048]{1,0:T(8,128)(2,1)}, bf16[64,2048]{1,0:T(8,128)(2,1)}, u32[]{:S(2)}, u32[]{:S(2)}) %collective-permute-start.51) | collective-permute-done | bytes 262176 | tf_op jit(solution)/shard_map/ppermute | solution.py:214
  285.6 2.9 %fusion.69 = bf16[128,2048]{1,0:T(8,128)(2,1)} fusion(bf16[128,2048]{1,0:T(8,128)(2,1)} %copy-done.4, bf16[128,2048]{1,0:T(8,128)(2,1)} %collective-permute-done.54, bf16[128,2048]{1,0:T(8,128)(2,1)} %collective-permute-done.47, bf16[2,128,2048]{2,1,0:T(8,128)(2,1)} %copy-done.9, bf16[64,2048]{1,0:T(8,128)(2,1)} %collective-permute-done.53, ...), kind=kLoop, calls=%fused_computation.95 | loop fusion | flops 3407872 | bytes 3145728 | tf_op jit(solution)/shard_map/convert_element_type | solution.py:627
  (222 shorter events, 76.6 us)
Async XLA Ops:
  2.7 15.3 %collective-permute-start = (bf16[2048,128]{1,0:T(8,128)(2,1)}, bf16[2048,128]{1,0:T(8,128)(2,1)}, u32[]{:S(2)}, u32[]{:S(2)}) collective-permute-start(bf16[2048,128]{1,0:T(8,128)(2,1)} %constant_dynamic-slice_fusion.1), channel_id=1, source_target_pairs={{0,1},{1,0},{2,3},{3,2},{4,5},{5,4},{6,7},{7,6},{8,9},{9,8},{10,11... | collective-permute-start | bytes 1572872 | tf_op jit(solution)/shard_map/ppermute | solution.py:214
  7.0 13.0 %collective-permute-start.1 = (bf16[16,128]{1,0:T(8,128)(2,1)S(1)}, bf16[16,128]{1,0:T(8,128)(2,1)S(1)}, u32[]{:S(2)}, u32[]{:S(2)}) collective-permute-start(bf16[16,128]{1,0:T(8,128)(2,1)S(1)} %pad_maximum_fusion.20), channel_id=1, source_target_pairs={{0,16},{1,17},{2,18},{3,19},{4,20},{5,21},{6,22},{7,23},{8,24},{9,... | collective-permute-start | bytes 12296 | tf_op jit(solution)/shard_map/ppermute | solution.py:214
  8.5 31.8 %collective-permute-start.6 = (bf16[128,2048]{1,0:T(8,128)(2,1)}, bf16[128,2048]{1,0:T(8,128)(2,1)}, u32[]{:S(2)}, u32[]{:S(2)}) collective-permute-start(bf16[128,2048]{1,0:T(8,128)(2,1)} %tokens.1), channel_id=1, source_target_pairs={{0,4},{1,5},{2,6},{3,7},{4,0},{5,1},{6,2},{7,3},{8,12},{9,13},{10,... | collective-permute-start | bytes 1572872 | tf_op jit(solution)/shard_map/ppermute | solution.py:214
  20.1 16.4 %collective-permute-start.4 = (bf16[144,256]{1,0:T(8,128)(2,1)S(1)}, bf16[144,256]{1,0:T(8,128)(2,1)S(1)}, u32[]{:S(2)}, u32[]{:S(2)}) collective-permute-start(bf16[144,256]{1,0:T(8,128)(2,1)S(1)} %get-tuple-element.194), channel_id=1, source_target_pairs={{0,6},{1,7},{2,4},{3,5},{4,2},{5,3},{6,0},{7,1},{8,14},{9,15},{10,... | collective-permute-start | bytes 221192 | tf_op jit(solution)/shard_map/ppermute | solution.py:214
  23.9 16.4 %collective-permute-start.3 = (bf16[144,256]{1,0:T(8,128)(2,1)S(1)}, bf16[144,256]{1,0:T(8,128)(2,1)S(1)}, u32[]{:S(2)}, u32[]{:S(2)}) collective-permute-start(bf16[144,256]{1,0:T(8,128)(2,1)S(1)} %get-tuple-element.193), channel_id=1, source_target_pairs={{0,4},{1,5},{2,6},{3,7},{4,0},{5,1},{6,2},{7,3},{8,12},{9,13},{10,... | collective-permute-start | bytes 221192 | tf_op jit(solution)/shard_map/ppermute | solution.py:214
  23.9 12.3 %collective-permute-start.2 = (bf16[144,256]{1,0:T(8,128)(2,1)S(1)}, bf16[144,256]{1,0:T(8,128)(2,1)S(1)}, u32[]{:S(2)}, u32[]{:S(2)}) collective-permute-start(bf16[144,256]{1,0:T(8,128)(2,1)S(1)} %get-tuple-element.192), channel_id=1, source_target_pairs={{0,2},{1,3},{2,0},{3,1},{4,6},{5,7},{6,4},{7,5},{8,10},{9,11},{10,... | collective-permute-start | bytes 221192 | tf_op jit(solution)/shard_map/ppermute | solution.py:214
  25.6 14.7 %collective-permute-start.5 = (bf16[128,2048]{1,0:T(8,128)(2,1)S(1)}, bf16[128,2048]{1,0:T(8,128)(2,1)S(1)}, u32[]{:S(2)}, u32[]{:S(2)}) collective-permute-start(bf16[128,2048]{1,0:T(8,128)(2,1)S(1)} %constant_dynamic-slice_fusion), channel_id=1, source_target_pairs={{0,1},{1,0},{2,3},{3,2},{4,5},{5,4},{6,7},{7,6},{8,9},{9,8},{10,11... | collective-permute-start | bytes 1572872 | tf_op jit(solution)/shard_map/ppermute | solution.py:214
  36.2 9.9 %collective-permute-start.9 = (bf16[2048,128]{1,0:T(8,128)(2,1)}, bf16[2048,128]{1,0:T(8,128)(2,1)S(1)}, u32[]{:S(2)}, u32[]{:S(2)}) collective-permute-start(bf16[2048,128]{1,0:T(8,128)(2,1)} %collective-permute-done), channel_id=1, source_target_pairs={{0,16},{1,17},{2,18},{3,19},{4,20},{5,21},{6,22},{7,23},{8,24},{9,... | collective-permute-start | bytes 1572872 | tf_op jit(solution)/shard_map/ppermute | solution.py:214
  41.0 11.0 %collective-permute-start.7 = (bf16[4,144,256]{2,1,0:T(8,128)(2,1)S(1)}, bf16[4,144,256]{2,1,0:T(8,128)(2,1)S(1)}, u32[]{:S(2)}, u32[]{:S(2)}) collective-permute-start(bf16[4,144,256]{2,1,0:T(8,128)(2,1)S(1)} %pad_maximum_fusion.15.kv_here), channel_id=1, source_target_pairs={{0,8},{8,16},{16,24},{1,9},{9,17},{17,25},{2,10},{10,18},{18,26},{... | collective-permute-start | bytes 884744 | tf_op jit(solution)/shard_map/ppermute | solution.py:15
  43.9 14.7 %collective-permute-start.11 = (bf16[128,2048]{1,0:T(8,128)(2,1)}, bf16[128,2048]{1,0:T(8,128)(2,1)S(1)}, u32[]{:S(2)}, u32[]{:S(2)}) collective-permute-start(bf16[128,2048]{1,0:T(8,128)(2,1)} %collective-permute-done.6), channel_id=1, source_target_pairs={{0,2},{1,3},{2,0},{3,1},{4,6},{5,7},{6,4},{7,5},{8,10},{9,11},{10,... | collective-permute-start | bytes 1572872 | tf_op jit(solution)/shard_map/ppermute | solution.py:214
  45.1 14.5 %collective-permute-start.12 = (bf16[128,2048]{1,0:T(8,128)(2,1)S(1)}, bf16[128,2048]{1,0:T(8,128)(2,1)S(1)}, u32[]{:S(2)}, u32[]{:S(2)}) collective-permute-start(bf16[128,2048]{1,0:T(8,128)(2,1)S(1)} %collective-permute-done.5), channel_id=1, source_target_pairs={{0,16},{1,17},{2,18},{3,19},{4,20},{5,21},{6,22},{7,23},{8,24},{9,... | collective-permute-start | bytes 1572872 | tf_op jit(solution)/shard_map/ppermute | solution.py:214
  49.2 10.4 %collective-permute-start.10 = (bf16[2048,256]{1,0:T(8,128)(2,1)S(1)}, bf16[2048,256]{1,0:T(8,128)(2,1)S(1)}, u32[]{:S(2)}, u32[]{:S(2)}) collective-permute-start(bf16[2048,256]{1,0:T(8,128)(2,1)S(1)} %pad_maximum_fusion.6), channel_id=1, source_target_pairs={{0,8},{1,9},{2,10},{3,11},{4,12},{5,13},{6,14},{7,15},{8,0},{9,1},... | collective-permute-start | bytes 3145736 | tf_op jit(solution)/shard_map/ppermute | solution.py:214
  49.2 15.7 %collective-permute-start.13 = (bf16[4,144,256]{2,1,0:T(8,128)(2,1)S(1)}, bf16[4,144,256]{2,1,0:T(8,128)(2,1)S(1)}, u32[]{:S(2)}, u32[]{:S(2)}) collective-permute-start(bf16[4,144,256]{2,1,0:T(8,128)(2,1)S(1)} %collective-permute-done.8.kv_side), channel_id=1, source_target_pairs={{0,8},{8,16},{16,24},{1,9},{9,17},{17,25},{2,10},{10,18},{18,26},{... | collective-permute-start | bytes 884744 | tf_op jit(solution)/shard_map/ppermute | solution.py:15
  61.1 14.8 %collective-permute-start.15 = (bf16[128,2048]{1,0:T(8,128)(2,1)S(1)}, bf16[128,2048]{1,0:T(8,128)(2,1)S(1)}, u32[]{:S(2)}, u32[]{:S(2)}) collective-permute-start(bf16[128,2048]{1,0:T(8,128)(2,1)S(1)} %copy-done.5), channel_id=1, source_target_pairs={{0,2},{1,3},{2,0},{3,1},{4,6},{5,7},{6,4},{7,5},{8,10},{9,11},{10,... | collective-permute-start | bytes 1572872 | tf_op jit(solution)/shard_map/ppermute | solution.py:214
  71.8 15.3 %collective-permute-start.17 = (bf16[128,2048]{1,0:T(8,128)(2,1)S(1)}, bf16[128,2048]{1,0:T(8,128)(2,1)S(1)}, u32[]{:S(2)}, u32[]{:S(2)}) collective-permute-start(bf16[128,2048]{1,0:T(8,128)(2,1)S(1)} %get-tuple-element.153), channel_id=1, source_target_pairs={{0,2},{1,3},{2,0},{3,1},{4,6},{5,7},{6,4},{7,5},{8,10},{9,11},{10,... | collective-permute-start | bytes 1572872 | tf_op jit(solution)/shard_map/ppermute | solution.py:214
  83.0 25.0 %collective-permute-start.16 = (bf16[128,2048]{1,0:T(8,128)(2,1)S(1)}, bf16[128,2048]{1,0:T(8,128)(2,1)S(1)}, u32[]{:S(2)}, u32[]{:S(2)}) collective-permute-start(bf16[128,2048]{1,0:T(8,128)(2,1)S(1)} %slice.349), channel_id=1, source_target_pairs={{0,2},{1,3},{2,0},{3,1},{4,6},{5,7},{6,4},{7,5},{8,10},{9,11},{10,... | collective-permute-start | bytes 1572872 | tf_op jit(solution)/shard_map/ppermute | solution.py:214
  87.3 25.8 %collective-permute-start.18 = (bf16[128,2048]{1,0:T(8,128)(2,1)S(1)}, bf16[128,2048]{1,0:T(8,128)(2,1)S(1)}, u32[]{:S(2)}, u32[]{:S(2)}) collective-permute-start(bf16[128,2048]{1,0:T(8,128)(2,1)S(1)} %add_convert_fusion.1), channel_id=1, source_target_pairs={{0,4},{1,5},{2,6},{3,7},{4,0},{5,1},{6,2},{7,3},{8,12},{9,13},{10,... | collective-permute-start | bytes 1572872 | tf_op jit(solution)/shard_map/ppermute | solution.py:214
  113.8 11.3 %collective-permute-start.21 = (bf16[128,2048]{1,0:T(8,128)(2,1)S(1)}, bf16[128,2048]{1,0:T(8,128)(2,1)S(1)}, u32[]{:S(2)}, u32[]{:S(2)}) collective-permute-start(bf16[128,2048]{1,0:T(8,128)(2,1)S(1)} %fusion.65), channel_id=1, source_target_pairs={{0,1},{1,0},{2,3},{3,2},{4,5},{5,4},{6,7},{7,6},{8,9},{9,8},{10,11... | collective-permute-start | bytes 1572872 | tf_op jit(solution)/shard_map/ppermute | solution.py:214
  115.3 12.0 %collective-permute-start.22 = (bf16[128,2048]{1,0:T(8,128)(2,1)S(1)}, bf16[128,2048]{1,0:T(8,128)(2,1)S(1)}, u32[]{:S(2)}, u32[]{:S(2)}) collective-permute-start(bf16[128,2048]{1,0:T(8,128)(2,1)S(1)} %fusion.65), channel_id=1, source_target_pairs={{0,16},{1,17},{2,18},{3,19},{4,20},{5,21},{6,22},{7,23},{8,24},{9,... | collective-permute-start | bytes 1572872 | tf_op jit(solution)/shard_map/ppermute | solution.py:214
  116.9 20.6 %collective-permute-start.19 = (bf16[128,2048]{1,0:T(8,128)(2,1)S(1)}, bf16[128,2048]{1,0:T(8,128)(2,1)S(1)}, u32[]{:S(2)}, u32[]{:S(2)}) collective-permute-start(bf16[128,2048]{1,0:T(8,128)(2,1)S(1)} %fusion.65), channel_id=1, source_target_pairs={{0,2},{1,3},{2,0},{3,1},{4,6},{5,7},{6,4},{7,5},{8,10},{9,11},{10,... | collective-permute-start | bytes 1572872 | tf_op jit(solution)/shard_map/ppermute | solution.py:214
  117.0 23.4 %collective-permute-start.20 = (bf16[128,2048]{1,0:T(8,128)(2,1)S(1)}, bf16[128,2048]{1,0:T(8,128)(2,1)S(1)}, u32[]{:S(2)}, u32[]{:S(2)}) collective-permute-start(bf16[128,2048]{1,0:T(8,128)(2,1)S(1)} %fusion.65), channel_id=1, source_target_pairs={{0,4},{1,5},{2,6},{3,7},{4,0},{5,1},{6,2},{7,3},{8,12},{9,13},{10,... | collective-permute-start | bytes 1572872 | tf_op jit(solution)/shard_map/ppermute | solution.py:214
  127.3 13.0 %collective-permute-start.23 = (bf16[64,2048]{1,0:T(8,128)(2,1)S(1)}, bf16[64,2048]{1,0:T(8,128)(2,1)S(1)}, u32[]{:S(2)}, u32[]{:S(2)}) collective-permute-start(bf16[64,2048]{1,0:T(8,128)(2,1)S(1)} %slice.285), channel_id=1, source_target_pairs={{0,16},{1,17},{2,18},{3,19},{4,20},{5,21},{6,22},{7,23},{8,24},{9,... | collective-permute-start | bytes 786440 | tf_op jit(solution)/shard_map/ppermute | solution.py:214
  128.6 11.8 %collective-permute-start.24 = (bf16[64,2048]{1,0:T(8,128)(2,1)S(1)}, bf16[64,2048]{1,0:T(8,128)(2,1)S(1)}, u32[]{:S(2)}, u32[]{:S(2)}) collective-permute-start(bf16[64,2048]{1,0:T(8,128)(2,1)S(1)} %slice.286), channel_id=1, source_target_pairs={{0,1},{1,0},{2,3},{3,2},{4,5},{5,4},{6,7},{7,6},{8,9},{9,8},{10,11... | collective-permute-start | bytes 786440 | tf_op jit(solution)/shard_map/ppermute | solution.py:214
  141.2 10.4 %collective-permute-start.28 = (bf16[128,2048]{1,0:T(8,128)(2,1)S(1)}, bf16[128,2048]{1,0:T(8,128)(2,1)S(1)}, u32[]{:S(2)}, u32[]{:S(2)}) collective-permute-start(bf16[128,2048]{1,0:T(8,128)(2,1)S(1)} %collective-permute-done.19), channel_id=1, source_target_pairs={{0,16},{1,17},{2,18},{3,19},{4,20},{5,21},{6,22},{7,23},{8,24},{9,... | collective-permute-start | bytes 1572872 | tf_op jit(solution)/shard_map/ppermute | solution.py:214
  152.4 14.4 %collective-permute-start.27 = (bf16[128,2048]{1,0:T(8,128)(2,1)S(1)}, bf16[128,2048]{1,0:T(8,128)(2,1)S(1)}, u32[]{:S(2)}, u32[]{:S(2)}) collective-permute-start(bf16[128,2048]{1,0:T(8,128)(2,1)S(1)} %collective-permute-done.26), channel_id=1, source_target_pairs={{0,16},{1,17},{2,18},{3,19},{4,20},{5,21},{6,22},{7,23},{8,24},{9,... | collective-permute-start | bytes 1572872 | tf_op jit(solution)/shard_map/ppermute | solution.py:214
  154.7 19.7 %collective-permute-start.34 = (bf16[2,96,2048]{2,1,0:T(8,128)(2,1)S(1)}, bf16[2,96,2048]{2,1,0:T(8,128)(2,1)S(1)}, u32[]{:S(2)}, u32[]{:S(2)}) collective-permute-start(bf16[2,96,2048]{2,1,0:T(8,128)(2,1)S(1)} %slice.367), channel_id=1, source_target_pairs={{0,1},{1,0},{2,3},{3,2},{4,5},{5,4},{6,7},{7,6},{8,9},{9,8},{10,11... | collective-permute-start | bytes 2359304 | tf_op jit(solution)/shard_map/ppermute | solution.py:214
  166.9 12.1 %collective-permute-start.32 = (bf16[2,48,2048]{2,1,0:T(8,128)(2,1)S(1)}, bf16[2,48,2048]{2,1,0:T(8,128)(2,1)S(1)}, u32[]{:S(2)}, u32[]{:S(2)}) collective-permute-start(bf16[2,48,2048]{2,1,0:T(8,128)(2,1)S(1)} %get-tuple-element.159), channel_id=1, source_target_pairs={{0,16},{1,17},{2,18},{3,19},{4,20},{5,21},{6,22},{7,23},{8,24},{9,... | collective-permute-start | bytes 1179656 | tf_op jit(solution)/shard_map/ppermute | solution.py:214
  168.7 16.7 %collective-permute-start.33 = (bf16[2,48,2048]{2,1,0:T(8,128)(2,1)S(1)}, bf16[2,48,2048]{2,1,0:T(8,128)(2,1)S(1)}, u32[]{:S(2)}, u32[]{:S(2)}) collective-permute-start(bf16[2,48,2048]{2,1,0:T(8,128)(2,1)S(1)} %get-tuple-element.158), channel_id=1, source_target_pairs={{0,24},{1,25},{2,26},{3,27},{4,28},{5,29},{6,30},{7,31},{8,16},{9,... | collective-permute-start | bytes 1179656 | tf_op jit(solution)/shard_map/ppermute | solution.py:214
  174.5 12.1 %collective-permute-start.35 = (bf16[2,48,2048]{2,1,0:T(8,128)(2,1)S(1)}, bf16[2,48,2048]{2,1,0:T(8,128)(2,1)S(1)}, u32[]{:S(2)}, u32[]{:S(2)}) collective-permute-start(bf16[2,48,2048]{2,1,0:T(8,128)(2,1)S(1)} %get-tuple-element.157), channel_id=1, source_target_pairs={{0,1},{1,0},{2,3},{3,2},{4,5},{5,4},{6,7},{7,6},{8,9},{9,8},{10,11... | collective-permute-start | bytes 1179656 | tf_op jit(solution)/shard_map/ppermute | solution.py:214
  176.0 16.4 %collective-permute-start.36 = (bf16[2,48,2048]{2,1,0:T(8,128)(2,1)S(1)}, bf16[2,48,2048]{2,1,0:T(8,128)(2,1)S(1)}, u32[]{:S(2)}, u32[]{:S(2)}) collective-permute-start(bf16[2,48,2048]{2,1,0:T(8,128)(2,1)S(1)} %get-tuple-element.156), channel_id=1, source_target_pairs={{0,9},{1,8},{2,11},{3,10},{4,13},{5,12},{6,15},{7,14},{8,1},{9,0},... | collective-permute-start | bytes 1179656 | tf_op jit(solution)/shard_map/ppermute | solution.py:214
  176.2 16.3 %collective-permute-start.37 = (bf16[4,48,2048]{2,1,0:T(8,128)(2,1)S(1)}, bf16[4,48,2048]{2,1,0:T(8,128)(2,1)S(1)}, u32[]{:S(2)}, u32[]{:S(2)}) collective-permute-start(bf16[4,48,2048]{2,1,0:T(8,128)(2,1)S(1)} %pad_maximum_fusion.12), channel_id=1, source_target_pairs={{0,8},{1,9},{2,10},{3,11},{4,12},{5,13},{6,14},{7,15},{8,0},{9,1},... | collective-permute-start | bytes 2359304 | tf_op jit(solution)/shard_map/ppermute | solution.py:214
  179.0 26.1 %collective-permute-start.31 = (bf16[4,48,2048]{2,1,0:T(8,128)(2,1)S(1)}, bf16[4,48,2048]{2,1,0:T(8,128)(2,1)S(1)}, u32[]{:S(2)}, u32[]{:S(2)}) collective-permute-start(bf16[4,48,2048]{2,1,0:T(8,128)(2,1)S(1)} %get-tuple-element.134), channel_id=1, source_target_pairs={{0,8},{1,9},{2,10},{3,11},{4,12},{5,13},{6,14},{7,15},{8,0},{9,1},... | collective-permute-start | bytes 2359304 | tf_op jit(solution)/shard_map/ppermute | solution.py:214
  196.9 12.1 %collective-permute-start.38 = (bf16[2,48,2048]{2,1,0:T(8,128)(2,1)S(1)}, bf16[2,48,2048]{2,1,0:T(8,128)(2,1)S(1)}, u32[]{:S(2)}, u32[]{:S(2)}) collective-permute-start(bf16[2,48,2048]{2,1,0:T(8,128)(2,1)S(1)} %get-tuple-element.139), channel_id=1, source_target_pairs={{0,16},{1,17},{2,18},{3,19},{4,20},{5,21},{6,22},{7,23},{8,24},{9,... | collective-permute-start | bytes 1179656 | tf_op jit(solution)/shard_map/ppermute | solution.py:214
  197.2 19.8 %collective-permute-start.39 = (bf16[2,48,2048]{2,1,0:T(8,128)(2,1)S(1)}, bf16[2,48,2048]{2,1,0:T(8,128)(2,1)S(1)}, u32[]{:S(2)}, u32[]{:S(2)}) collective-permute-start(bf16[2,48,2048]{2,1,0:T(8,128)(2,1)S(1)} %get-tuple-element.138), channel_id=1, source_target_pairs={{0,24},{1,25},{2,26},{3,27},{4,28},{5,29},{6,30},{7,31},{8,16},{9,... | collective-permute-start | bytes 1179656 | tf_op jit(solution)/shard_map/ppermute | solution.py:214
  199.1 17.9 %collective-permute-start.40 = (bf16[2,48,2048]{2,1,0:T(8,128)(2,1)S(1)}, bf16[2,48,2048]{2,1,0:T(8,128)(2,1)S(1)}, u32[]{:S(2)}, u32[]{:S(2)}) collective-permute-start(bf16[2,48,2048]{2,1,0:T(8,128)(2,1)S(1)} %get-tuple-element.137), channel_id=1, source_target_pairs={{0,1},{1,0},{2,3},{3,2},{4,5},{5,4},{6,7},{7,6},{8,9},{9,8},{10,11... | collective-permute-start | bytes 1179656 | tf_op jit(solution)/shard_map/ppermute | solution.py:214
  200.6 17.0 %collective-permute-start.41 = (bf16[2,48,2048]{2,1,0:T(8,128)(2,1)S(1)}, bf16[2,48,2048]{2,1,0:T(8,128)(2,1)S(1)}, u32[]{:S(2)}, u32[]{:S(2)}) collective-permute-start(bf16[2,48,2048]{2,1,0:T(8,128)(2,1)S(1)} %get-tuple-element.136), channel_id=1, source_target_pairs={{0,9},{1,8},{2,11},{3,10},{4,13},{5,12},{6,15},{7,14},{8,1},{9,0},... | collective-permute-start | bytes 1179656 | tf_op jit(solution)/shard_map/ppermute | solution.py:214
  205.1 13.8 %collective-permute-start.43 = (bf16[4,48,2048]{2,1,0:T(8,128)(2,1)S(1)}, bf16[4,48,2048]{2,1,0:T(8,128)(2,1)S(1)}, u32[]{:S(2)}, u32[]{:S(2)}) collective-permute-start(bf16[4,48,2048]{2,1,0:T(8,128)(2,1)S(1)} %bitcast.204), channel_id=1, source_target_pairs={{0,8},{1,9},{2,10},{3,11},{4,12},{5,13},{6,14},{7,15},{8,0},{9,1},... | collective-permute-start | bytes 2359304 | tf_op jit(solution)/shard_map/ppermute | solution.py:214
  209.0 11.9 %collective-permute-start.45 = (bf16[4,48,2048]{2,1,0:T(8,128)(2,1)S(1)}, bf16[4,48,2048]{2,1,0:T(8,128)(2,1)S(1)}, u32[]{:S(2)}, u32[]{:S(2)}) collective-permute-start(bf16[4,48,2048]{2,1,0:T(8,128)(2,1)S(1)} %get-tuple-element.141), channel_id=1, source_target_pairs={{0,8},{1,9},{2,10},{3,11},{4,12},{5,13},{6,14},{7,15},{8,0},{9,1},... | collective-permute-start | bytes 2359304 | tf_op jit(solution)/shard_map/ppermute | solution.py:214
  218.1 14.7 %collective-permute-start.42 = (bf16[128,2048]{1,0:T(8,128)(2,1)S(1)}, bf16[128,2048]{1,0:T(8,128)(2,1)S(1)}, u32[]{:S(2)}, u32[]{:S(2)}) collective-permute-start(bf16[128,2048]{1,0:T(8,128)(2,1)S(1)} %slice_bitcast_fusion.4), channel_id=1, source_target_pairs={{0,1},{1,0},{2,3},{3,2},{4,5},{5,4},{6,7},{7,6},{8,9},{9,8},{10,11... | collective-permute-start | bytes 1572872 | tf_op jit(solution)/shard_map/ppermute | solution.py:214
  219.6 14.6 %collective-permute-start.44 = (bf16[128,2048]{1,0:T(8,128)(2,1)S(1)}, bf16[128,2048]{1,0:T(8,128)(2,1)S(1)}, u32[]{:S(2)}, u32[]{:S(2)}) collective-permute-start(bf16[128,2048]{1,0:T(8,128)(2,1)S(1)} %slice_bitcast_fusion.3), channel_id=1, source_target_pairs={{0,16},{1,17},{2,18},{3,19},{4,20},{5,21},{6,22},{7,23},{8,24},{9,... | collective-permute-start | bytes 1572872 | tf_op jit(solution)/shard_map/ppermute | solution.py:214
  234.3 13.7 %collective-permute-start.46 = (bf16[128,2048]{1,0:T(8,128)(2,1)S(1)}, bf16[128,2048]{1,0:T(8,128)(2,1)S(1)}, u32[]{:S(2)}, u32[]{:S(2)}) collective-permute-start(bf16[128,2048]{1,0:T(8,128)(2,1)S(1)} %fusion.83), channel_id=1, source_target_pairs={{0,2},{1,3},{2,0},{3,1},{4,6},{5,7},{6,4},{7,5},{8,10},{9,11},{10,... | collective-permute-start | bytes 1572872 | tf_op jit(solution)/shard_map/ppermute | solution.py:214
  235.2 19.0 %collective-permute-start.48 = (bf16[2,96,2048]{2,1,0:T(8,128)(2,1)S(1)}, bf16[2,96,2048]{2,1,0:T(8,128)(2,1)S(1)}, u32[]{:S(2)}, u32[]{:S(2)}) collective-permute-start(bf16[2,96,2048]{2,1,0:T(8,128)(2,1)S(1)} %fusion.93), channel_id=1, source_target_pairs={{0,16},{1,17},{2,18},{3,19},{4,20},{5,21},{6,22},{7,23},{8,24},{9,... | collective-permute-start | bytes 2359304 | tf_op jit(solution)/shard_map/ppermute | solution.py:214
  236.2 18.6 %collective-permute-start.49 = (bf16[2,96,2048]{2,1,0:T(8,128)(2,1)S(1)}, bf16[2,96,2048]{2,1,0:T(8,128)(2,1)S(1)}, u32[]{:S(2)}, u32[]{:S(2)}) collective-permute-start(bf16[2,96,2048]{2,1,0:T(8,128)(2,1)S(1)} %get-tuple-element.117), channel_id=1, source_target_pairs={{0,1},{1,0},{2,3},{3,2},{4,5},{5,4},{6,7},{7,6},{8,9},{9,8},{10,11... | collective-permute-start | bytes 2359304 | tf_op jit(solution)/shard_map/ppermute | solution.py:214
  249.1 26.3 %collective-permute-start.47 = (bf16[128,2048]{1,0:T(8,128)(2,1)}, bf16[128,2048]{1,0:T(8,128)(2,1)}, u32[]{:S(2)}, u32[]{:S(2)}) collective-permute-start(bf16[128,2048]{1,0:T(8,128)(2,1)} %fusion.85), channel_id=1, source_target_pairs={{0,4},{1,5},{2,6},{3,7},{4,0},{5,1},{6,2},{7,3},{8,12},{9,13},{10,... | collective-permute-start | bytes 1572872 | tf_op jit(solution)/shard_map/ppermute | solution.py:214
  256.6 10.8 %collective-permute-start.52 = (bf16[64,2048]{1,0:T(8,128)(2,1)S(1)}, bf16[64,2048]{1,0:T(8,128)(2,1)S(1)}, u32[]{:S(2)}, u32[]{:S(2)}) collective-permute-start(bf16[64,2048]{1,0:T(8,128)(2,1)S(1)} %get-tuple-element.151), channel_id=1, source_target_pairs={{0,16},{1,17},{2,18},{3,19},{4,20},{5,21},{6,22},{7,23},{8,24},{9,... | collective-permute-start | bytes 786440 | tf_op jit(solution)/shard_map/ppermute | solution.py:214
  258.8 16.6 %collective-permute-start.54 = (bf16[128,2048]{1,0:T(8,128)(2,1)}, bf16[128,2048]{1,0:T(8,128)(2,1)}, u32[]{:S(2)}, u32[]{:S(2)}) collective-permute-start(bf16[128,2048]{1,0:T(8,128)(2,1)} %slice_bitcast_fusion), channel_id=1, source_target_pairs={{0,1},{1,0},{2,3},{3,2},{4,5},{5,4},{6,7},{7,6},{8,9},{9,8},{10,11... | collective-permute-start | bytes 1572872 | tf_op jit(solution)/shard_map/ppermute | solution.py:214
  268.3 11.7 %collective-permute-start.53 = (bf16[64,2048]{1,0:T(8,128)(2,1)}, bf16[64,2048]{1,0:T(8,128)(2,1)}, u32[]{:S(2)}, u32[]{:S(2)}) collective-permute-start(bf16[64,2048]{1,0:T(8,128)(2,1)} %get-tuple-element.149), channel_id=1, source_target_pairs={{0,2},{1,3},{2,0},{3,1},{4,6},{5,7},{6,4},{7,5},{8,10},{9,11},{10,... | collective-permute-start | bytes 786440 | tf_op jit(solution)/shard_map/ppermute | solution.py:214
  269.5 16.1 %collective-permute-start.51 = (bf16[64,2048]{1,0:T(8,128)(2,1)}, bf16[64,2048]{1,0:T(8,128)(2,1)}, u32[]{:S(2)}, u32[]{:S(2)}) collective-permute-start(bf16[64,2048]{1,0:T(8,128)(2,1)} %get-tuple-element.148), channel_id=1, source_target_pairs={{0,2},{1,3},{2,0},{3,1},{4,6},{5,7},{6,4},{7,5},{8,10},{9,11},{10,... | collective-permute-start | bytes 786440 | tf_op jit(solution)/shard_map/ppermute | solution.py:214
  (24 other events, 381.9 us)
where the time goes:
time: 290 us; the launch traced here: 288 us
  waiting for transfers between devices  156 us (54%)
  starting transfers between devices  59.9 us (21%)
  matrix products  27.5 us (9%)
  other arithmetic  15 us (5%)
  Pallas kernels  14.6 us (5%)
  local copies, waits for them, and re-layouts  14 us (5%)
    ppermute x53, waiting for transfers between devices, moved(): return lax.ppermute(block, ('rep', 'tp'), route)  156 us
    ppermute x53, starting transfers between devices, moved(): return lax.ppermute(block, ('rep', 'tp'), route)  56.2 us
    dot_general x4, matrix products, experts_of(): jnp.dot(slot_rows_in, w_gate_up[0], preferred_element_type=jnp.float32)  10.6 us
    pallas_call x2, Pallas kernels, attend_slots(): pl.pallas_call(functools.partial(attention_kernel, first_slot), grid_spec...  9.43 us
    dot_general x4, matrix products, experts_of(): jnp.dot(act, w_down[0], preferred_element_type=jnp.float32)  5.85 us
  transfers between devices with their start and end apart: 55, of which 34 were waited for; matrix products, arithmetic and copies ran while one was open for 17% of the time, Pallas kernels for 5%

commit v1 on v0

--- a/solution.py
+++ b/solution.py
@@ -617,9 +617,9 @@
     far = own_2.astype(jnp.float32) + side_2.astype(jnp.float32) + far_3.astype(jnp.float32)
     far = other_z(far.astype(jnp.bfloat16), 2)
     side_0 = other_x(side_0)
-    near = [
-        other_z(sum_of(own_1[part], other_y(side_1[part])), 1) for part in (slice(0, half), slice(half, rows))
-    ]
+    near, later = sum_of(own_1[:half], other_y(side_1[:half])), other_y(side_1[half:])
+    near, later = together(near, later)
+    near = [other_z(near, 1), other_z(sum_of(own_1[half:], later), 1)]
     near = jnp.concatenate(near, axis=0)
     combined = residual.astype(jnp.float32)
     for value in (far, near, own_0, side_0):

time: 290 us -> 293 us (1.010)
  waiting for transfers between devices: 156 us -> 163 us
  starting transfers between devices: 59.9 us -> 56.4 us
    ppermute x53, waiting for transfers between devices: 156 us -> 163 us  [moved(): return lax.ppermute(block, ('rep', 'tp'), route)]
    ppermute x53, starting transfers between devices: 56.2 us -> 52.7 us  [moved(): return lax.ppermute(block, ('rep', 'tp'), route)]
  transfers between devices with their start and end apart: 55 -> 55, of which waited for: 34 -> 34; matrix products, arithmetic and copies ran while one was open for 17% -> 18% of each run, Pallas kernels for 5% -> 5%
where the time goes in v1:
time: 293 us; the launch traced here: 292 us
  waiting for transfers between devices  163 us (56%)
  starting transfers between devices  56.4 us (19%)
  matrix products  27.4 us (9%)
  other arithmetic  15.6 us (5%)
  local copies, waits for them, and re-layouts  14 us (5%)
  Pallas kernels  14 us (5%)
    ppermute x53, waiting for transfers between devices, moved(): return lax.ppermute(block, ('rep', 'tp'), route)  163 us
    ppermute x53, starting transfers between devices, moved(): return lax.ppermute(block, ('rep', 'tp'), route)  52.7 us
    dot_general x4, matrix products, experts_of(): jnp.dot(slot_rows_in, w_gate_up[0], preferred_element_type=jnp.float32)  10.6 us
    pallas_call x2, Pallas kernels, attend_slots(): pl.pallas_call(functools.partial(attention_kernel, first_slot), grid_spec...  8.75 us
  transfers between devices with their start and end apart: 55, of which 34 were waited for; matrix products, arithmetic and copies ran while one was open for 18% of the time, Pallas kernels for 5%

profile of v1, /device:TPU:0, one launch (start us, length us, event | category | flops | bytes accessed | tf_op | source)
XLA Modules:
  0.0 291.9 jit_solution(11228499638238858101)
XLA Ops:
  0.7 2.0 constant_dynamic-slice_fusion.1
  2.7 2.9 %collective-permute-start = (bf16[2048,128]{1,0:T(8,128)(2,1)}, bf16[2048,128]{1,0:T(8,128)(2,1)}, u32[]{:S(2)}, u32[]{:S(2)}) collective-permute-start(bf16[2048,128]{1,0:T(8,128)(2,1)} %constant_dynamic-slice_fusion.1), channel_id=1, source_target_pairs={{0,1},{1,0},{2,3},{3,2},{4,5},{5,4},{6,7},{7,6},{8,9},{9,8},{10,11... | collective-permute-start | bytes 1572872 | tf_op jit(solution)/shard_map/ppermute | solution.py:214
  7.0 1.5 collective-permute-start.1
  8.5 2.6 collective-permute-start.6
  12.7 5.2 %keyval.1 = bf16[4,128,256]{2,1,0:T(8,128)(2,1)} custom-call(bf16[128,2048]{1,0:T(8,128)(2,1)} %tokens.1, f32[1,2048]{1,0:T(1,128)} %bitcast.225, f32[1,128]{1,0:T(1,128)} %bitcast.226, f32[4,64,128]{2,1,0:T(8,128)} %get-tuple-element.198.cosine, f32[4,64,128]{2,1,0:T(8,128)} %get-tuple-element.197.sine, bf16[2048,1024]{1,0:T(8,128)(2,1)} %w_value.1, ...), custom_call_target="tpu_custom_call" | custom-call | flops 536870912 | bytes 5242880 | tf_op jit(solution)/shard_map/keyval/pallas_call | solution.py:373
  20.1 3.8 %collective-permute-start.4 = (bf16[144,256]{1,0:T(8,128)(2,1)S(1)}, bf16[144,256]{1,0:T(8,128)(2,1)S(1)}, u32[]{:S(2)}, u32[]{:S(2)}) collective-permute-start(bf16[144,256]{1,0:T(8,128)(2,1)S(1)} %get-tuple-element.196), channel_id=1, source_target_pairs={{0,6},{1,7},{2,4},{3,5},{4,2},{5,3},{6,0},{7,1},{8,14},{9,15},{10,... | collective-permute-start | bytes 221192 | tf_op jit(solution)/shard_map/ppermute | solution.py:214
  25.6 1.7 collective-permute-start.5
  27.5 8.7 %collective-permute-done.2 = bf16[144,256]{1,0:T(8,128)(2,1)S(1)} collective-permute-done((bf16[144,256]{1,0:T(8,128)(2,1)S(1)}, bf16[144,256]{1,0:T(8,128)(2,1)S(1)}, u32[]{:S(2)}, u32[]{:S(2)}) %collective-permute-start.2) | collective-permute-done | bytes 73760 | tf_op jit(solution)/shard_map/ppermute | solution.py:214
  36.5 3.8 %collective-permute-done.3 = bf16[144,256]{1,0:T(8,128)(2,1)S(1)} collective-permute-done((bf16[144,256]{1,0:T(8,128)(2,1)S(1)}, bf16[144,256]{1,0:T(8,128)(2,1)S(1)}, u32[]{:S(2)}, u32[]{:S(2)}) %collective-permute-start.3) | collective-permute-done | bytes 73760 | tf_op jit(solution)/shard_map/ppermute | solution.py:214
  46.1 1.9 collective-permute-done.8.kv_side
  49.2 2.4 collective-permute-start.13
  51.9 6.7 %collective-permute-done.11 = bf16[128,2048]{1,0:T(8,128)(2,1)S(1)} collective-permute-done((bf16[128,2048]{1,0:T(8,128)(2,1)}, bf16[128,2048]{1,0:T(8,128)(2,1)S(1)}, u32[]{:S(2)}, u32[]{:S(2)}) %collective-permute-start.11) | collective-permute-done | bytes 524320 | tf_op jit(solution)/shard_map/ppermute | solution.py:214
  62.5 2.4 fusion.72.projected
  65.0 4.6 %attention.2 = bf16[256,1024]{1,0:T(8,128)(2,1)S(1)} custom-call(s32[2]{0:T(128)S(1)} %pad_add_fusion.1.place, s32[4]{0:T(128)S(1)} %and_select_fusion.low, f32[256,1024]{1,0:T(8,128)S(1)} %fusion.72.projected, f32[1,128]{1,0:T(1,128)S(1)} %bitcast.192, f32[4,64,128]{2,1,0:T(8,128)S(1)} %copy-done.2, f32[4,64,128]{2,1,0:T(8,128)S(1)} %copy-done.1, ...), custom_call_target="tpu_custom_call" | custom-call | flops 536870912 | bytes 8388608 | tf_op jit(solution)/shard_map/attention/pallas_call | solution.py:316
  72.1 3.4 %collective-permute-done.15 = bf16[128,2048]{1,0:T(8,128)(2,1)S(1)} collective-permute-done((bf16[128,2048]{1,0:T(8,128)(2,1)S(1)}, bf16[128,2048]{1,0:T(8,128)(2,1)S(1)}, u32[]{:S(2)}, u32[]{:S(2)}) %collective-permute-start.15) | collective-permute-done | bytes 524320 | tf_op jit(solution)/shard_map/ppermute | solution.py:214
  77.1 4.1 %attention.3 = bf16[256,1024]{1,0:T(8,128)(2,1)S(1)} custom-call(s32[2]{0:T(128)S(1)} %pad_add_fusion.1.place, s32[4]{0:T(128)S(1)} %and_select_fusion.low, f32[256,1024]{1,0:T(8,128)S(1)} %fusion.70.projected, f32[1,128]{1,0:T(1,128)S(1)} %bitcast.193, f32[4,64,128]{2,1,0:T(8,128)S(1)} %copy-done.2, f32[4,64,128]{2,1,0:T(8,128)S(1)} %copy-done.1, ...), custom_call_target="tpu_custom_call" | custom-call | flops 536870912 | bytes 8388608 | tf_op jit(solution)/shard_map/attention/pallas_call | solution.py:316
  83.7 2.4 collective-permute-done.17
  86.2 3.8 %collective-permute-start.18 = (bf16[128,2048]{1,0:T(8,128)(2,1)S(1)}, bf16[128,2048]{1,0:T(8,128)(2,1)S(1)}, u32[]{:S(2)}, u32[]{:S(2)}) collective-permute-start(bf16[128,2048]{1,0:T(8,128)(2,1)S(1)} %add_convert_fusion.1), channel_id=1, source_target_pairs={{0,4},{1,5},{2,6},{3,7},{4,0},{5,1},{6,2},{7,3},{8,12},{9,13},{10,... | collective-permute-start | bytes 1572872 | tf_op jit(solution)/shard_map/ppermute | solution.py:214
  90.6 16.2 %collective-permute-done.16 = bf16[128,2048]{1,0:T(8,128)(2,1)S(1)} collective-permute-done((bf16[128,2048]{1,0:T(8,128)(2,1)S(1)}, bf16[128,2048]{1,0:T(8,128)(2,1)S(1)}, u32[]{:S(2)}, u32[]{:S(2)}) %collective-permute-start.16) | collective-permute-done | bytes 524320 | tf_op jit(solution)/shard_map/ppermute | solution.py:214
  106.8 6.7 %collective-permute-done.18 = bf16[128,2048]{1,0:T(8,128)(2,1)S(1)} collective-permute-done((bf16[128,2048]{1,0:T(8,128)(2,1)S(1)}, bf16[128,2048]{1,0:T(8,128)(2,1)S(1)}, u32[]{:S(2)}, u32[]{:S(2)}) %collective-permute-start.18) | collective-permute-done | bytes 524320 | tf_op jit(solution)/shard_map/ppermute | solution.py:214
  114.2 1.7 collective-permute-start.21
  116.5 2.6 collective-permute-start.20
  119.4 8.3 %collective-permute-done.21 = bf16[128,2048]{1,0:T(8,128)(2,1)S(1)} collective-permute-done((bf16[128,2048]{1,0:T(8,128)(2,1)S(1)}, bf16[128,2048]{1,0:T(8,128)(2,1)S(1)}, u32[]{:S(2)}, u32[]{:S(2)}) %collective-permute-start.21) | collective-permute-done | bytes 524320 | tf_op jit(solution)/shard_map/ppermute | solution.py:214
  130.0 10.6 %collective-permute-done.19 = bf16[128,2048]{1,0:T(8,128)(2,1)S(1)} collective-permute-done((bf16[128,2048]{1,0:T(8,128)(2,1)S(1)}, bf16[128,2048]{1,0:T(8,128)(2,1)S(1)}, u32[]{:S(2)}, u32[]{:S(2)}) %collective-permute-start.19) | collective-permute-done | bytes 524320 | tf_op jit(solution)/shard_map/ppermute | solution.py:214
  142.9 1.8 collective-permute-start.28
  145.4 8.1 %collective-permute-done.25 = bf16[128,2048]{1,0:T(8,128)(2,1)S(1)} collective-permute-done((bf16[128,2048]{1,0:T(8,128)(2,1)S(1)}, bf16[128,2048]{1,0:T(8,128)(2,1)S(1)}, u32[]{:S(2)}, u32[]{:S(2)}) %collective-permute-start.25) | collective-permute-done | bytes 524320 | tf_op jit(solution)/shard_map/ppermute | solution.py:214
  159.7 2.7 fusion.6
  162.5 2.6 fusion.4
  168.1 2.4 collective-permute-done.27
  173.0 4.7 %collective-permute-done.34 = bf16[2,96,2048]{2,1,0:T(8,128)(2,1)S(1)} collective-permute-done((bf16[2,96,2048]{2,1,0:T(8,128)(2,1)S(1)}, bf16[2,96,2048]{2,1,0:T(8,128)(2,1)S(1)}, u32[]{:S(2)}, u32[]{:S(2)}) %collective-permute-start.34) | collective-permute-done | bytes 786464 | tf_op jit(solution)/shard_map/ppermute | solution.py:214
  177.8 1.6 collective-permute-start.35
  180.6 2.0 collective-permute-done.32
  182.7 6.1 %collective-permute-done.33 = bf16[2,48,2048]{2,1,0:T(8,128)(2,1)S(1)} collective-permute-done((bf16[2,48,2048]{2,1,0:T(8,128)(2,1)S(1)}, bf16[2,48,2048]{2,1,0:T(8,128)(2,1)S(1)}, u32[]{:S(2)}, u32[]{:S(2)}) %collective-permute-start.33) | collective-permute-done | bytes 393248 | tf_op jit(solution)/shard_map/ppermute | solution.py:214
  189.9 5.9 %collective-permute-done.36 = bf16[2,48,2048]{2,1,0:T(8,128)(2,1)S(1)} collective-permute-done((bf16[2,48,2048]{2,1,0:T(8,128)(2,1)S(1)}, bf16[2,48,2048]{2,1,0:T(8,128)(2,1)S(1)}, u32[]{:S(2)}, u32[]{:S(2)}) %collective-permute-start.36) | collective-permute-done | bytes 393248 | tf_op jit(solution)/shard_map/ppermute | solution.py:214
  196.1 2.6 fusion.2
  200.9 1.5 collective-permute-start.39
  204.2 2.6 fusion
  209.2 3.1 %collective-permute-done.38 = bf16[2,48,2048]{2,1,0:T(8,128)(2,1)S(1)} collective-permute-done((bf16[2,48,2048]{2,1,0:T(8,128)(2,1)S(1)}, bf16[2,48,2048]{2,1,0:T(8,128)(2,1)S(1)}, u32[]{:S(2)}, u32[]{:S(2)}) %collective-permute-start.38) | collective-permute-done | bytes 393248 | tf_op jit(solution)/shard_map/ppermute | solution.py:214
  212.3 8.1 %collective-permute-done.39 = bf16[2,48,2048]{2,1,0:T(8,128)(2,1)S(1)} collective-permute-done((bf16[2,48,2048]{2,1,0:T(8,128)(2,1)S(1)}, bf16[2,48,2048]{2,1,0:T(8,128)(2,1)S(1)}, u32[]{:S(2)}, u32[]{:S(2)}) %collective-permute-start.39) | collective-permute-done | bytes 393248 | tf_op jit(solution)/shard_map/ppermute | solution.py:214
  224.0 12.1 %collective-permute-done.42 = bf16[128,2048]{1,0:T(8,128)(2,1)S(1)} collective-permute-done((bf16[128,2048]{1,0:T(8,128)(2,1)S(1)}, bf16[128,2048]{1,0:T(8,128)(2,1)S(1)}, u32[]{:S(2)}, u32[]{:S(2)}) %collective-permute-start.42) | collective-permute-done | bytes 524320 | tf_op jit(solution)/shard_map/ppermute | solution.py:214
  240.2 11.2 %collective-permute-done.46 = bf16[128,2048]{1,0:T(8,128)(2,1)S(1)} collective-permute-done((bf16[128,2048]{1,0:T(8,128)(2,1)S(1)}, bf16[128,2048]{1,0:T(8,128)(2,1)S(1)}, u32[]{:S(2)}, u32[]{:S(2)}) %collective-permute-start.46) | collective-permute-done | bytes 524320 | tf_op jit(solution)/shard_map/ppermute | solution.py:214
  253.2 4.4 %collective-permute-done.48 = bf16[2,96,2048]{2,1,0:T(8,128)(2,1)S(1)} collective-permute-done((bf16[2,96,2048]{2,1,0:T(8,128)(2,1)S(1)}, bf16[2,96,2048]{2,1,0:T(8,128)(2,1)S(1)}, u32[]{:S(2)}, u32[]{:S(2)}) %collective-permute-start.48) | collective-permute-done | bytes 786464 | tf_op jit(solution)/shard_map/ppermute | solution.py:214
  262.8 5.3 %collective-permute-done.50 = bf16[64,2048]{1,0:T(8,128)(2,1)S(1)} collective-permute-done((bf16[64,2048]{1,0:T(8,128)(2,1)S(1)}, bf16[64,2048]{1,0:T(8,128)(2,1)S(1)}, u32[]{:S(2)}, u32[]{:S(2)}) %collective-permute-start.50) | collective-permute-done | bytes 262176 | tf_op jit(solution)/shard_map/ppermute | solution.py:214
  268.9 2.1 collective-permute-done.51
  274.6 2.0 copy.31
  278.8 4.6 %collective-permute-done.53 = bf16[64,2048]{1,0:T(8,128)(2,1)} collective-permute-done((bf16[64,2048]{1,0:T(8,128)(2,1)}, bf16[64,2048]{1,0:T(8,128)(2,1)}, u32[]{:S(2)}, u32[]{:S(2)}) %collective-permute-start.53) | collective-permute-done | bytes 262176 | tf_op jit(solution)/shard_map/ppermute | solution.py:214
  283.5 5.5 %collective-permute-done.52 = bf16[64,2048]{1,0:T(8,128)(2,1)} collective-permute-done((bf16[64,2048]{1,0:T(8,128)(2,1)}, bf16[64,2048]{1,0:T(8,128)(2,1)}, u32[]{:S(2)}, u32[]{:S(2)}) %collective-permute-start.52) | collective-permute-done | bytes 262176 | tf_op jit(solution)/shard_map/ppermute | solution.py:214
  289.0 2.9 fusion.69
  (223 shorter events, 74.0 us)
Async XLA Ops:
  2.7 15.3 %collective-permute-start = (bf16[2048,128]{1,0:T(8,128)(2,1)}, bf16[2048,128]{1,0:T(8,128)(2,1)}, u32[]{:S(2)}, u32[]{:S(2)}) collective-permute-start(bf16[2048,128]{1,0:T(8,128)(2,1)} %constant_dynamic-slice_fusion.1), channel_id=1, source_target_pairs={{0,1},{1,0},{2,3},{3,2},{4,5},{5,4},{6,7},{7,6},{8,9},{9,8},{10,11... | collective-permute-start | bytes 1572872 | tf_op jit(solution)/shard_map/ppermute | solution.py:214
  7.0 13.1 %collective-permute-start.1 = (bf16[16,128]{1,0:T(8,128)(2,1)S(1)}, bf16[16,128]{1,0:T(8,128)(2,1)S(1)}, u32[]{:S(2)}, u32[]{:S(2)}) collective-permute-start(bf16[16,128]{1,0:T(8,128)(2,1)S(1)} %pad_maximum_fusion.20), channel_id=1, source_target_pairs={{0,16},{1,17},{2,18},{3,19},{4,20},{5,21},{6,22},{7,23},{8,24},{9,... | collective-permute-start | bytes 12296 | tf_op jit(solution)/shard_map/ppermute | solution.py:214
  8.5 31.8 %collective-permute-start.6 = (bf16[128,2048]{1,0:T(8,128)(2,1)}, bf16[128,2048]{1,0:T(8,128)(2,1)}, u32[]{:S(2)}, u32[]{:S(2)}) collective-permute-start(bf16[128,2048]{1,0:T(8,128)(2,1)} %tokens.1), channel_id=1, source_target_pairs={{0,4},{1,5},{2,6},{3,7},{4,0},{5,1},{6,2},{7,3},{8,12},{9,13},{10,... | collective-permute-start | bytes 1572872 | tf_op jit(solution)/shard_map/ppermute | solution.py:214
  20.1 16.4 %collective-permute-start.4 = (bf16[144,256]{1,0:T(8,128)(2,1)S(1)}, bf16[144,256]{1,0:T(8,128)(2,1)S(1)}, u32[]{:S(2)}, u32[]{:S(2)}) collective-permute-start(bf16[144,256]{1,0:T(8,128)(2,1)S(1)} %get-tuple-element.196), channel_id=1, source_target_pairs={{0,6},{1,7},{2,4},{3,5},{4,2},{5,3},{6,0},{7,1},{8,14},{9,15},{10,... | collective-permute-start | bytes 221192 | tf_op jit(solution)/shard_map/ppermute | solution.py:214
  23.9 16.4 %collective-permute-start.3 = (bf16[144,256]{1,0:T(8,128)(2,1)S(1)}, bf16[144,256]{1,0:T(8,128)(2,1)S(1)}, u32[]{:S(2)}, u32[]{:S(2)}) collective-permute-start(bf16[144,256]{1,0:T(8,128)(2,1)S(1)} %get-tuple-element.195), channel_id=1, source_target_pairs={{0,4},{1,5},{2,6},{3,7},{4,0},{5,1},{6,2},{7,3},{8,12},{9,13},{10,... | collective-permute-start | bytes 221192 | tf_op jit(solution)/shard_map/ppermute | solution.py:214
  23.9 12.3 %collective-permute-start.2 = (bf16[144,256]{1,0:T(8,128)(2,1)S(1)}, bf16[144,256]{1,0:T(8,128)(2,1)S(1)}, u32[]{:S(2)}, u32[]{:S(2)}) collective-permute-start(bf16[144,256]{1,0:T(8,128)(2,1)S(1)} %get-tuple-element.194), channel_id=1, source_target_pairs={{0,2},{1,3},{2,0},{3,1},{4,6},{5,7},{6,4},{7,5},{8,10},{9,11},{10,... | collective-permute-start | bytes 221192 | tf_op jit(solution)/shard_map/ppermute | solution.py:214
  25.6 14.7 %collective-permute-start.5 = (bf16[128,2048]{1,0:T(8,128)(2,1)S(1)}, bf16[128,2048]{1,0:T(8,128)(2,1)S(1)}, u32[]{:S(2)}, u32[]{:S(2)}) collective-permute-start(bf16[128,2048]{1,0:T(8,128)(2,1)S(1)} %constant_dynamic-slice_fusion), channel_id=1, source_target_pairs={{0,1},{1,0},{2,3},{3,2},{4,5},{5,4},{6,7},{7,6},{8,9},{9,8},{10,11... | collective-permute-start | bytes 1572872 | tf_op jit(solution)/shard_map/ppermute | solution.py:214
  41.0 11.0 %collective-permute-start.7 = (bf16[4,144,256]{2,1,0:T(8,128)(2,1)S(1)}, bf16[4,144,256]{2,1,0:T(8,128)(2,1)S(1)}, u32[]{:S(2)}, u32[]{:S(2)}) collective-permute-start(bf16[4,144,256]{2,1,0:T(8,128)(2,1)S(1)} %pad_maximum_fusion.15.kv_here), channel_id=1, source_target_pairs={{0,8},{8,16},{16,24},{1,9},{9,17},{17,25},{2,10},{10,18},{18,26},{... | collective-permute-start | bytes 884744 | tf_op jit(solution)/shard_map/ppermute | solution.py:15
  43.9 14.7 %collective-permute-start.11 = (bf16[128,2048]{1,0:T(8,128)(2,1)}, bf16[128,2048]{1,0:T(8,128)(2,1)S(1)}, u32[]{:S(2)}, u32[]{:S(2)}) collective-permute-start(bf16[128,2048]{1,0:T(8,128)(2,1)} %collective-permute-done.6), channel_id=1, source_target_pairs={{0,2},{1,3},{2,0},{3,1},{4,6},{5,7},{6,4},{7,5},{8,10},{9,11},{10,... | collective-permute-start | bytes 1572872 | tf_op jit(solution)/shard_map/ppermute | solution.py:214
  45.1 14.5 %collective-permute-start.12 = (bf16[128,2048]{1,0:T(8,128)(2,1)S(1)}, bf16[128,2048]{1,0:T(8,128)(2,1)S(1)}, u32[]{:S(2)}, u32[]{:S(2)}) collective-permute-start(bf16[128,2048]{1,0:T(8,128)(2,1)S(1)} %collective-permute-done.5), channel_id=1, source_target_pairs={{0,16},{1,17},{2,18},{3,19},{4,20},{5,21},{6,22},{7,23},{8,24},{9,... | collective-permute-start | bytes 1572872 | tf_op jit(solution)/shard_map/ppermute | solution.py:214
  49.2 10.4 %collective-permute-start.10 = (bf16[2048,256]{1,0:T(8,128)(2,1)S(1)}, bf16[2048,256]{1,0:T(8,128)(2,1)S(1)}, u32[]{:S(2)}, u32[]{:S(2)}) collective-permute-start(bf16[2048,256]{1,0:T(8,128)(2,1)S(1)} %pad_maximum_fusion.6), channel_id=1, source_target_pairs={{0,8},{1,9},{2,10},{3,11},{4,12},{5,13},{6,14},{7,15},{8,0},{9,1},... | collective-permute-start | bytes 3145736 | tf_op jit(solution)/shard_map/ppermute | solution.py:214
  49.2 15.7 %collective-permute-start.13 = (bf16[4,144,256]{2,1,0:T(8,128)(2,1)S(1)}, bf16[4,144,256]{2,1,0:T(8,128)(2,1)S(1)}, u32[]{:S(2)}, u32[]{:S(2)}) collective-permute-start(bf16[4,144,256]{2,1,0:T(8,128)(2,1)S(1)} %collective-permute-done.8.kv_side), channel_id=1, source_target_pairs={{0,8},{8,16},{16,24},{1,9},{9,17},{17,25},{2,10},{10,18},{18,26},{... | collective-permute-start | bytes 884744 | tf_op jit(solution)/shard_map/ppermute | solution.py:15
  61.1 14.3 %collective-permute-start.15 = (bf16[128,2048]{1,0:T(8,128)(2,1)S(1)}, bf16[128,2048]{1,0:T(8,128)(2,1)S(1)}, u32[]{:S(2)}, u32[]{:S(2)}) collective-permute-start(bf16[128,2048]{1,0:T(8,128)(2,1)S(1)} %copy-done.5), channel_id=1, source_target_pairs={{0,2},{1,3},{2,0},{3,1},{4,6},{5,7},{6,4},{7,5},{8,10},{9,11},{10,... | collective-permute-start | bytes 1572872 | tf_op jit(solution)/shard_map/ppermute | solution.py:214
  71.2 14.9 %collective-permute-start.17 = (bf16[128,2048]{1,0:T(8,128)(2,1)S(1)}, bf16[128,2048]{1,0:T(8,128)(2,1)S(1)}, u32[]{:S(2)}, u32[]{:S(2)}) collective-permute-start(bf16[128,2048]{1,0:T(8,128)(2,1)S(1)} %get-tuple-element.155), channel_id=1, source_target_pairs={{0,2},{1,3},{2,0},{3,1},{4,6},{5,7},{6,4},{7,5},{8,10},{9,11},{10,... | collective-permute-start | bytes 1572872 | tf_op jit(solution)/shard_map/ppermute | solution.py:214
  82.5 24.3 %collective-permute-start.16 = (bf16[128,2048]{1,0:T(8,128)(2,1)S(1)}, bf16[128,2048]{1,0:T(8,128)(2,1)S(1)}, u32[]{:S(2)}, u32[]{:S(2)}) collective-permute-start(bf16[128,2048]{1,0:T(8,128)(2,1)S(1)} %slice.349), channel_id=1, source_target_pairs={{0,2},{1,3},{2,0},{3,1},{4,6},{5,7},{6,4},{7,5},{8,10},{9,11},{10,... | collective-permute-start | bytes 1572872 | tf_op jit(solution)/shard_map/ppermute | solution.py:214
  86.2 27.3 %collective-permute-start.18 = (bf16[128,2048]{1,0:T(8,128)(2,1)S(1)}, bf16[128,2048]{1,0:T(8,128)(2,1)S(1)}, u32[]{:S(2)}, u32[]{:S(2)}) collective-permute-start(bf16[128,2048]{1,0:T(8,128)(2,1)S(1)} %add_convert_fusion.1), channel_id=1, source_target_pairs={{0,4},{1,5},{2,6},{3,7},{4,0},{5,1},{6,2},{7,3},{8,12},{9,13},{10,... | collective-permute-start | bytes 1572872 | tf_op jit(solution)/shard_map/ppermute | solution.py:214
  114.2 13.5 %collective-permute-start.21 = (bf16[128,2048]{1,0:T(8,128)(2,1)S(1)}, bf16[128,2048]{1,0:T(8,128)(2,1)S(1)}, u32[]{:S(2)}, u32[]{:S(2)}) collective-permute-start(bf16[128,2048]{1,0:T(8,128)(2,1)S(1)} %fusion.65), channel_id=1, source_target_pairs={{0,1},{1,0},{2,3},{3,2},{4,5},{5,4},{6,7},{7,6},{8,9},{9,8},{10,11... | collective-permute-start | bytes 1572872 | tf_op jit(solution)/shard_map/ppermute | solution.py:214
  115.9 13.2 %collective-permute-start.22 = (bf16[128,2048]{1,0:T(8,128)(2,1)S(1)}, bf16[128,2048]{1,0:T(8,128)(2,1)S(1)}, u32[]{:S(2)}, u32[]{:S(2)}) collective-permute-start(bf16[128,2048]{1,0:T(8,128)(2,1)S(1)} %fusion.65), channel_id=1, source_target_pairs={{0,16},{1,17},{2,18},{3,19},{4,20},{5,21},{6,22},{7,23},{8,24},{9,... | collective-permute-start | bytes 1572872 | tf_op jit(solution)/shard_map/ppermute | solution.py:214
  116.4 24.2 %collective-permute-start.19 = (bf16[128,2048]{1,0:T(8,128)(2,1)S(1)}, bf16[128,2048]{1,0:T(8,128)(2,1)S(1)}, u32[]{:S(2)}, u32[]{:S(2)}) collective-permute-start(bf16[128,2048]{1,0:T(8,128)(2,1)S(1)} %fusion.65), channel_id=1, source_target_pairs={{0,2},{1,3},{2,0},{3,1},{4,6},{5,7},{6,4},{7,5},{8,10},{9,11},{10,... | collective-permute-start | bytes 1572872 | tf_op jit(solution)/shard_map/ppermute | solution.py:214
  116.5 25.4 %collective-permute-start.20 = (bf16[128,2048]{1,0:T(8,128)(2,1)S(1)}, bf16[128,2048]{1,0:T(8,128)(2,1)S(1)}, u32[]{:S(2)}, u32[]{:S(2)}) collective-permute-start(bf16[128,2048]{1,0:T(8,128)(2,1)S(1)} %fusion.65), channel_id=1, source_target_pairs={{0,4},{1,5},{2,6},{3,7},{4,0},{5,1},{6,2},{7,3},{8,12},{9,13},{10,... | collective-permute-start | bytes 1572872 | tf_op jit(solution)/shard_map/ppermute | solution.py:214
  129.1 12.7 %collective-permute-start.23 = (bf16[64,2048]{1,0:T(8,128)(2,1)S(1)}, bf16[64,2048]{1,0:T(8,128)(2,1)S(1)}, u32[]{:S(2)}, u32[]{:S(2)}) collective-permute-start(bf16[64,2048]{1,0:T(8,128)(2,1)S(1)} %slice.285), channel_id=1, source_target_pairs={{0,16},{1,17},{2,18},{3,19},{4,20},{5,21},{6,22},{7,23},{8,24},{9,... | collective-permute-start | bytes 786440 | tf_op jit(solution)/shard_map/ppermute | solution.py:214
  129.5 12.4 %collective-permute-start.24 = (bf16[64,2048]{1,0:T(8,128)(2,1)S(1)}, bf16[64,2048]{1,0:T(8,128)(2,1)S(1)}, u32[]{:S(2)}, u32[]{:S(2)}) collective-permute-start(bf16[64,2048]{1,0:T(8,128)(2,1)S(1)} %slice.286), channel_id=1, source_target_pairs={{0,1},{1,0},{2,3},{3,2},{4,5},{5,4},{6,7},{7,6},{8,9},{9,8},{10,11... | collective-permute-start | bytes 786440 | tf_op jit(solution)/shard_map/ppermute | solution.py:214
  141.9 11.6 %collective-permute-start.25 = (bf16[128,2048]{1,0:T(8,128)(2,1)S(1)}, bf16[128,2048]{1,0:T(8,128)(2,1)S(1)}, u32[]{:S(2)}, u32[]{:S(2)}) collective-permute-start(bf16[128,2048]{1,0:T(8,128)(2,1)S(1)} %collective-permute-done.20), channel_id=1, source_target_pairs={{0,1},{1,0},{2,3},{3,2},{4,5},{5,4},{6,7},{7,6},{8,9},{9,8},{10,11... | collective-permute-start | bytes 1572872 | tf_op jit(solution)/shard_map/ppermute | solution.py:214
  142.4 11.2 %collective-permute-start.26 = (bf16[128,2048]{1,0:T(8,128)(2,1)S(1)}, bf16[128,2048]{1,0:T(8,128)(2,1)S(1)}, u32[]{:S(2)}, u32[]{:S(2)}) collective-permute-start(bf16[128,2048]{1,0:T(8,128)(2,1)S(1)} %collective-permute-done.20), channel_id=1, source_target_pairs={{0,2},{1,3},{2,0},{3,1},{4,6},{5,7},{6,4},{7,5},{8,10},{9,11},{10,... | collective-permute-start | bytes 1572872 | tf_op jit(solution)/shard_map/ppermute | solution.py:214
  142.9 12.3 %collective-permute-start.28 = (bf16[128,2048]{1,0:T(8,128)(2,1)S(1)}, bf16[128,2048]{1,0:T(8,128)(2,1)S(1)}, u32[]{:S(2)}, u32[]{:S(2)}) collective-permute-start(bf16[128,2048]{1,0:T(8,128)(2,1)S(1)} %collective-permute-done.19), channel_id=1, source_target_pairs={{0,16},{1,17},{2,18},{3,19},{4,20},{5,21},{6,22},{7,23},{8,24},{9,... | collective-permute-start | bytes 1572872 | tf_op jit(solution)/shard_map/ppermute | solution.py:214
  156.1 14.4 %collective-permute-start.27 = (bf16[128,2048]{1,0:T(8,128)(2,1)S(1)}, bf16[128,2048]{1,0:T(8,128)(2,1)S(1)}, u32[]{:S(2)}, u32[]{:S(2)}) collective-permute-start(bf16[128,2048]{1,0:T(8,128)(2,1)S(1)} %collective-permute-done.26), channel_id=1, source_target_pairs={{0,16},{1,17},{2,18},{3,19},{4,20},{5,21},{6,22},{7,23},{8,24},{9,... | collective-permute-start | bytes 1572872 | tf_op jit(solution)/shard_map/ppermute | solution.py:214
  158.0 19.7 %collective-permute-start.34 = (bf16[2,96,2048]{2,1,0:T(8,128)(2,1)S(1)}, bf16[2,96,2048]{2,1,0:T(8,128)(2,1)S(1)}, u32[]{:S(2)}, u32[]{:S(2)}) collective-permute-start(bf16[2,96,2048]{2,1,0:T(8,128)(2,1)S(1)} %slice.367), channel_id=1, source_target_pairs={{0,1},{1,0},{2,3},{3,2},{4,5},{5,4},{6,7},{7,6},{8,9},{9,8},{10,11... | collective-permute-start | bytes 2359304 | tf_op jit(solution)/shard_map/ppermute | solution.py:214
  170.6 12.1 %collective-permute-start.32 = (bf16[2,48,2048]{2,1,0:T(8,128)(2,1)S(1)}, bf16[2,48,2048]{2,1,0:T(8,128)(2,1)S(1)}, u32[]{:S(2)}, u32[]{:S(2)}) collective-permute-start(bf16[2,48,2048]{2,1,0:T(8,128)(2,1)S(1)} %get-tuple-element.161), channel_id=1, source_target_pairs={{0,16},{1,17},{2,18},{3,19},{4,20},{5,21},{6,22},{7,23},{8,24},{9,... | collective-permute-start | bytes 1179656 | tf_op jit(solution)/shard_map/ppermute | solution.py:214
  172.1 16.7 %collective-permute-start.33 = (bf16[2,48,2048]{2,1,0:T(8,128)(2,1)S(1)}, bf16[2,48,2048]{2,1,0:T(8,128)(2,1)S(1)}, u32[]{:S(2)}, u32[]{:S(2)}) collective-permute-start(bf16[2,48,2048]{2,1,0:T(8,128)(2,1)S(1)} %get-tuple-element.160), channel_id=1, source_target_pairs={{0,24},{1,25},{2,26},{3,27},{4,28},{5,29},{6,30},{7,31},{8,16},{9,... | collective-permute-start | bytes 1179656 | tf_op jit(solution)/shard_map/ppermute | solution.py:214
  177.8 12.1 %collective-permute-start.35 = (bf16[2,48,2048]{2,1,0:T(8,128)(2,1)S(1)}, bf16[2,48,2048]{2,1,0:T(8,128)(2,1)S(1)}, u32[]{:S(2)}, u32[]{:S(2)}) collective-permute-start(bf16[2,48,2048]{2,1,0:T(8,128)(2,1)S(1)} %get-tuple-element.159), channel_id=1, source_target_pairs={{0,1},{1,0},{2,3},{3,2},{4,5},{5,4},{6,7},{7,6},{8,9},{9,8},{10,11... | collective-permute-start | bytes 1179656 | tf_op jit(solution)/shard_map/ppermute | solution.py:214
  179.4 16.4 %collective-permute-start.36 = (bf16[2,48,2048]{2,1,0:T(8,128)(2,1)S(1)}, bf16[2,48,2048]{2,1,0:T(8,128)(2,1)S(1)}, u32[]{:S(2)}, u32[]{:S(2)}) collective-permute-start(bf16[2,48,2048]{2,1,0:T(8,128)(2,1)S(1)} %get-tuple-element.158), channel_id=1, source_target_pairs={{0,9},{1,8},{2,11},{3,10},{4,13},{5,12},{6,15},{7,14},{8,1},{9,0},... | collective-permute-start | bytes 1179656 | tf_op jit(solution)/shard_map/ppermute | solution.py:214
  179.6 16.3 %collective-permute-start.37 = (bf16[4,48,2048]{2,1,0:T(8,128)(2,1)S(1)}, bf16[4,48,2048]{2,1,0:T(8,128)(2,1)S(1)}, u32[]{:S(2)}, u32[]{:S(2)}) collective-permute-start(bf16[4,48,2048]{2,1,0:T(8,128)(2,1)S(1)} %pad_maximum_fusion.12), channel_id=1, source_target_pairs={{0,8},{1,9},{2,10},{3,11},{4,12},{5,13},{6,14},{7,15},{8,0},{9,1},... | collective-permute-start | bytes 2359304 | tf_op jit(solution)/shard_map/ppermute | solution.py:214
  182.6 25.8 %collective-permute-start.31 = (bf16[4,48,2048]{2,1,0:T(8,128)(2,1)S(1)}, bf16[4,48,2048]{2,1,0:T(8,128)(2,1)S(1)}, u32[]{:S(2)}, u32[]{:S(2)}) collective-permute-start(bf16[4,48,2048]{2,1,0:T(8,128)(2,1)S(1)} %get-tuple-element.138), channel_id=1, source_target_pairs={{0,8},{1,9},{2,10},{3,11},{4,12},{5,13},{6,14},{7,15},{8,0},{9,1},... | collective-permute-start | bytes 2359304 | tf_op jit(solution)/shard_map/ppermute | solution.py:214
  200.3 12.1 %collective-permute-start.38 = (bf16[2,48,2048]{2,1,0:T(8,128)(2,1)S(1)}, bf16[2,48,2048]{2,1,0:T(8,128)(2,1)S(1)}, u32[]{:S(2)}, u32[]{:S(2)}) collective-permute-start(bf16[2,48,2048]{2,1,0:T(8,128)(2,1)S(1)} %get-tuple-element.143), channel_id=1, source_target_pairs={{0,16},{1,17},{2,18},{3,19},{4,20},{5,21},{6,22},{7,23},{8,24},{9,... | collective-permute-start | bytes 1179656 | tf_op jit(solution)/shard_map/ppermute | solution.py:214
  200.9 19.4 %collective-permute-start.39 = (bf16[2,48,2048]{2,1,0:T(8,128)(2,1)S(1)}, bf16[2,48,2048]{2,1,0:T(8,128)(2,1)S(1)}, u32[]{:S(2)}, u32[]{:S(2)}) collective-permute-start(bf16[2,48,2048]{2,1,0:T(8,128)(2,1)S(1)} %get-tuple-element.142), channel_id=1, source_target_pairs={{0,24},{1,25},{2,26},{3,27},{4,28},{5,29},{6,30},{7,31},{8,16},{9,... | collective-permute-start | bytes 1179656 | tf_op jit(solution)/shard_map/ppermute | solution.py:214
  202.5 17.9 %collective-permute-start.40 = (bf16[2,48,2048]{2,1,0:T(8,128)(2,1)S(1)}, bf16[2,48,2048]{2,1,0:T(8,128)(2,1)S(1)}, u32[]{:S(2)}, u32[]{:S(2)}) collective-permute-start(bf16[2,48,2048]{2,1,0:T(8,128)(2,1)S(1)} %get-tuple-element.141), channel_id=1, source_target_pairs={{0,1},{1,0},{2,3},{3,2},{4,5},{5,4},{6,7},{7,6},{8,9},{9,8},{10,11... | collective-permute-start | bytes 1179656 | tf_op jit(solution)/shard_map/ppermute | solution.py:214
  204.0 17.0 %collective-permute-start.41 = (bf16[2,48,2048]{2,1,0:T(8,128)(2,1)S(1)}, bf16[2,48,2048]{2,1,0:T(8,128)(2,1)S(1)}, u32[]{:S(2)}, u32[]{:S(2)}) collective-permute-start(bf16[2,48,2048]{2,1,0:T(8,128)(2,1)S(1)} %get-tuple-element.140), channel_id=1, source_target_pairs={{0,9},{1,8},{2,11},{3,10},{4,13},{5,12},{6,15},{7,14},{8,1},{9,0},... | collective-permute-start | bytes 1179656 | tf_op jit(solution)/shard_map/ppermute | solution.py:214
  208.4 13.9 %collective-permute-start.43 = (bf16[4,48,2048]{2,1,0:T(8,128)(2,1)S(1)}, bf16[4,48,2048]{2,1,0:T(8,128)(2,1)S(1)}, u32[]{:S(2)}, u32[]{:S(2)}) collective-permute-start(bf16[4,48,2048]{2,1,0:T(8,128)(2,1)S(1)} %bitcast.204), channel_id=1, source_target_pairs={{0,8},{1,9},{2,10},{3,11},{4,12},{5,13},{6,14},{7,15},{8,0},{9,1},... | collective-permute-start | bytes 2359304 | tf_op jit(solution)/shard_map/ppermute | solution.py:214
  212.3 11.7 %collective-permute-start.45 = (bf16[4,48,2048]{2,1,0:T(8,128)(2,1)S(1)}, bf16[4,48,2048]{2,1,0:T(8,128)(2,1)S(1)}, u32[]{:S(2)}, u32[]{:S(2)}) collective-permute-start(bf16[4,48,2048]{2,1,0:T(8,128)(2,1)S(1)} %get-tuple-element.145), channel_id=1, source_target_pairs={{0,8},{1,9},{2,10},{3,11},{4,12},{5,13},{6,14},{7,15},{8,0},{9,1},... | collective-permute-start | bytes 2359304 | tf_op jit(solution)/shard_map/ppermute | solution.py:214
  221.5 14.7 %collective-permute-start.42 = (bf16[128,2048]{1,0:T(8,128)(2,1)S(1)}, bf16[128,2048]{1,0:T(8,128)(2,1)S(1)}, u32[]{:S(2)}, u32[]{:S(2)}) collective-permute-start(bf16[128,2048]{1,0:T(8,128)(2,1)S(1)} %slice_bitcast_fusion.4), channel_id=1, source_target_pairs={{0,1},{1,0},{2,3},{3,2},{4,5},{5,4},{6,7},{7,6},{8,9},{9,8},{10,11... | collective-permute-start | bytes 1572872 | tf_op jit(solution)/shard_map/ppermute | solution.py:214
  223.0 14.6 %collective-permute-start.44 = (bf16[128,2048]{1,0:T(8,128)(2,1)S(1)}, bf16[128,2048]{1,0:T(8,128)(2,1)S(1)}, u32[]{:S(2)}, u32[]{:S(2)}) collective-permute-start(bf16[128,2048]{1,0:T(8,128)(2,1)S(1)} %slice_bitcast_fusion.3), channel_id=1, source_target_pairs={{0,16},{1,17},{2,18},{3,19},{4,20},{5,21},{6,22},{7,23},{8,24},{9,... | collective-permute-start | bytes 1572872 | tf_op jit(solution)/shard_map/ppermute | solution.py:214
  237.7 13.7 %collective-permute-start.46 = (bf16[128,2048]{1,0:T(8,128)(2,1)S(1)}, bf16[128,2048]{1,0:T(8,128)(2,1)S(1)}, u32[]{:S(2)}, u32[]{:S(2)}) collective-permute-start(bf16[128,2048]{1,0:T(8,128)(2,1)S(1)} %fusion.83), channel_id=1, source_target_pairs={{0,2},{1,3},{2,0},{3,1},{4,6},{5,7},{6,4},{7,5},{8,10},{9,11},{10,... | collective-permute-start | bytes 1572872 | tf_op jit(solution)/shard_map/ppermute | solution.py:214
  238.6 19.0 %collective-permute-start.48 = (bf16[2,96,2048]{2,1,0:T(8,128)(2,1)S(1)}, bf16[2,96,2048]{2,1,0:T(8,128)(2,1)S(1)}, u32[]{:S(2)}, u32[]{:S(2)}) collective-permute-start(bf16[2,96,2048]{2,1,0:T(8,128)(2,1)S(1)} %fusion.93), channel_id=1, source_target_pairs={{0,16},{1,17},{2,18},{3,19},{4,20},{5,21},{6,22},{7,23},{8,24},{9,... | collective-permute-start | bytes 2359304 | tf_op jit(solution)/shard_map/ppermute | solution.py:214
  239.6 18.7 %collective-permute-start.49 = (bf16[2,96,2048]{2,1,0:T(8,128)(2,1)S(1)}, bf16[2,96,2048]{2,1,0:T(8,128)(2,1)S(1)}, u32[]{:S(2)}, u32[]{:S(2)}) collective-permute-start(bf16[2,96,2048]{2,1,0:T(8,128)(2,1)S(1)} %get-tuple-element.119), channel_id=1, source_target_pairs={{0,1},{1,0},{2,3},{3,2},{4,5},{5,4},{6,7},{7,6},{8,9},{9,8},{10,11... | collective-permute-start | bytes 2359304 | tf_op jit(solution)/shard_map/ppermute | solution.py:214
  252.5 26.3 %collective-permute-start.47 = (bf16[128,2048]{1,0:T(8,128)(2,1)}, bf16[128,2048]{1,0:T(8,128)(2,1)}, u32[]{:S(2)}, u32[]{:S(2)}) collective-permute-start(bf16[128,2048]{1,0:T(8,128)(2,1)} %fusion.85), channel_id=1, source_target_pairs={{0,4},{1,5},{2,6},{3,7},{4,0},{5,1},{6,2},{7,3},{8,12},{9,13},{10,... | collective-permute-start | bytes 1572872 | tf_op jit(solution)/shard_map/ppermute | solution.py:214
  261.3 17.5 %collective-permute-start.54 = (bf16[128,2048]{1,0:T(8,128)(2,1)}, bf16[128,2048]{1,0:T(8,128)(2,1)}, u32[]{:S(2)}, u32[]{:S(2)}) collective-permute-start(bf16[128,2048]{1,0:T(8,128)(2,1)} %slice_bitcast_fusion), channel_id=1, source_target_pairs={{0,1},{1,0},{2,3},{3,2},{4,5},{5,4},{6,7},{7,6},{8,9},{9,8},{10,11... | collective-permute-start | bytes 1572872 | tf_op jit(solution)/shard_map/ppermute | solution.py:214
  271.8 11.7 %collective-permute-start.53 = (bf16[64,2048]{1,0:T(8,128)(2,1)}, bf16[64,2048]{1,0:T(8,128)(2,1)}, u32[]{:S(2)}, u32[]{:S(2)}) collective-permute-start(bf16[64,2048]{1,0:T(8,128)(2,1)} %fusion.104), channel_id=1, source_target_pairs={{0,2},{1,3},{2,0},{3,1},{4,6},{5,7},{6,4},{7,5},{8,10},{9,11},{10,... | collective-permute-start | bytes 786440 | tf_op jit(solution)/shard_map/ppermute | solution.py:214
  273.2 15.8 %collective-permute-start.52 = (bf16[64,2048]{1,0:T(8,128)(2,1)}, bf16[64,2048]{1,0:T(8,128)(2,1)}, u32[]{:S(2)}, u32[]{:S(2)}) collective-permute-start(bf16[64,2048]{1,0:T(8,128)(2,1)} %fusion.105), channel_id=1, source_target_pairs={{0,2},{1,3},{2,0},{3,1},{4,6},{5,7},{6,4},{7,5},{8,10},{9,11},{10,... | collective-permute-start | bytes 786440 | tf_op jit(solution)/shard_map/ppermute | solution.py:214
  (24 other events, 389.0 us)
